TPU v7x, 256 devices: a whole 4x4x8 slice. The times are simulated.
256 devices in a mesh: gx: 16 (over z, x_lo), gy: 4 (over y), gz: 4 (over x_hi, core).
Axes of the slice: x: 4 (x_hi: 2, x_lo: 2; x = x_hi * 2 + x_lo), y: 4, z: 8, core: 2. Of those that a mesh axis runs over, the one named last changes fastest.
Arguments:
- loads: float32 [16, 1048576], P(None, ('gx', 'gy', 'gz')), may hold values from -50 to 50
- displacement: float32 [1048576], P(('gx', 'gy', 'gz')), may hold values from -6 to 6
- stiffness: float32 [16384, 7, 4096], P(('gx', 'gy', 'gz')), may hold values from -100 to 300, as said below
- col_index: int32 [16384, 7], P(('gx', 'gy', 'gz')), may hold values from 0 to 159, as said below
- face_index: int32 [1536, 16], P(('gx', 'gy', 'gz')), may hold values from 0 to 63, as said below
- zone_map: int32 [16384, 6], P(('gx', 'gy', 'gz')), may hold values from 0 to 32767, as said below
Outputs:
- adjoint: float32 [16, 1048576], P(None, ('gx', 'gy', 'gz'))
- sensitivity: float32 [16, 32768], P(None, ('gx', 'gy', 'gz'))
Inputs may be any that keep to these rules, and one draw needn't show every extreme that they name: `col_index`: in each aligned block of 64 rows (one subdomain), entry 0 of row r is r, and entries 1 to 6 name the row's coupled node blocks in directions -x, +x, -y, +y, -z, +z: one of the same subdomain by its row within the block, one across a face by 64 + d * 16 + f, f being the row's position in that subdomain's face list for direction d. Block at position f of a face in direction d touches the block at position f of the neighbour's face in the opposite direction. `face_index`: row 6 * s + d lists, each once, the subdomain's node blocks (rows within its block of 64) on its face in direction d. `zone_map`: entries of subdomain s lie in zones s * 128 to s * 128 + 2 * 128 - 1, taken modulo 32768; both ends of this window occur in every subdomain. `stiffness`: the whole operator is symmetric positive definite; diagonal entries of the diagonal blocks are positive.
All inputs are finite; a program needn't handle non-finite values.
Results may differ from a plain program's by a relative error of at most 0.0003.
Values sent between devices are 32-bit elements; how exact they have to be, the bound alone decides.
A program may use at most 128 MiB of HBM per device.

v0:
```python
import jax
import jax.numpy as jnp
from jax import lax
from jax.sharding import PartitionSpec as P

ITERS = 2
ZONE_DEV = 128


def extended_2(cells, sides, width):
    for axis, dim in sides:
        count = lax.axis_size(axis)
        ends = count - 1
        head = lax.slice_in_dim(cells, 0, width, axis=dim)
        tail = lax.slice_in_dim(cells, cells.shape[dim] - width, cells.shape[dim], axis=dim)
        cells = jnp.concatenate(
            [
                lax.ppermute(tail, axis, [(i, (i + 1) % count) for i in range(ends)]),
                cells,
                lax.ppermute(head, axis, [((i + 1) % count, i) for i in range(ends)]),
            ],
            axis=dim,
        )
    return cells


def passed_along(value, axis, steps):
    count = lax.axis_size(axis)
    pairs = [(source, (source + steps) % count) for source in range(count)]
    return lax.ppermute(value, axis, pairs)


def inner_gram(left_in, right_in):
    return jnp.dot(left_in, right_in.T, precision=lax.Precision.HIGHEST)


def cho_apply(matrix_in, right_in):
    factor = jnp.linalg.cholesky(matrix_in)
    return jax.scipy.linalg.cho_solve((factor, True), right_in)


def total_gram(value):
    return lax.psum(value, ("gx", "gy", "gz"))


def on_device(loads, displacement, stiffness, col_index, face_index, zone_map):
    n_cols, local_dofs = loads.shape
    n_blocks = col_index.shape[0]
    block_dof = local_dofs // n_blocks
    face_size = face_index.shape[1]
    blocks = stiffness.reshape(n_blocks, 7, block_dof, block_dof)
    inverse_diag = (1.0 / jnp.diagonal(blocks[:, 0], axis1=1, axis2=2)).reshape(local_dofs)

    def split_faces(field_in):
        height = field_in.shape[0]
        blockwise = jnp.swapaxes(field_in.reshape(height, n_blocks, block_dof), 0, 1)
        sides = blockwise[face_index].reshape(6, face_size, height * block_dof)
        return (blockwise, sides)

    def stack_halos(along_x, along_y, along_z, height):
        halos = jnp.stack(
            [along_x[0], along_x[3], along_y[0], along_y[3], along_z[0], along_z[3]], axis=0
        )
        return halos.reshape(6 * face_size, height, block_dof)

    records = []
    adjoint = jnp.zeros_like(loads)
    residual = loads
    precond = residual * inverse_diag[None, :]
    direction = precond
    norm_gram = total_gram(inner_gram(residual, precond))
    for step in range(ITERS):
        apply_height = direction.shape[0]
        apply_blockwise, apply_sides = split_faces(direction)
        apply_along_x = extended_2(apply_sides[0:2], (("gx", 0),), 1)
        apply_along_y = extended_2(apply_sides[2:4], (("gy", 0),), 1)
        apply_along_z = extended_2(apply_sides[4:6], (("gz", 0),), 1)
        apply_halos = stack_halos(apply_along_x, apply_along_y, apply_along_z, apply_height)
        apply_extended = jnp.concatenate(
            [apply_blockwise[:, :n_cols], apply_halos[:, :n_cols]], axis=0
        )
        gathered = apply_extended[col_index]
        image = jnp.einsum("akij,akcj->cai", blocks, gathered, precision=lax.Precision.HIGHEST)
        image, halos = (image.reshape(n_cols, local_dofs), apply_halos)
        curvature = total_gram(inner_gram(direction, image))
        step_size = cho_apply(curvature, norm_gram)
        records.append((step_size, halos))
        adjoint = adjoint + jnp.dot(step_size.T, direction, precision=lax.Precision.HIGHEST)
        residual = residual - jnp.dot(step_size.T, image, precision=lax.Precision.HIGHEST)
        if step + 1 < ITERS:
            precond = residual * inverse_diag[None, :]
            next_gram = total_gram(inner_gram(residual, precond))
            mix_ratio = cho_apply(norm_gram, next_gram)
            direction = precond + jnp.dot(mix_ratio.T, direction, precision=lax.Precision.HIGHEST)
            norm_gram = next_gram
    stacked = jnp.concatenate([adjoint, displacement[None, :]], axis=0)
    blockwise, sides = split_faces(stacked)
    last_xs = extended_2(sides[0:2], (("gx", 0),), 1)
    last_ys = extended_2(sides[2:4], (("gy", 0),), 1)
    last_zs = extended_2(sides[4:6], (("gz", 0),), 1)
    extended = jnp.concatenate(
        [blockwise, stack_halos(last_xs, last_ys, last_zs, n_cols + 1)], axis=0
    )
    own_blocks = extended[:n_blocks]
    beside = extended[col_index[:, 1:]]
    differ = own_blocks[:, None] - beside
    moved = jnp.einsum(
        "akij,akj->aki", blocks[:, 1:], differ[:, :, n_cols], precision=lax.Precision.HIGHEST
    )
    contrib = 0.5 * jnp.einsum(
        "akci,aki->cak", differ[:, :, :n_cols], moved, precision=lax.Precision.HIGHEST
    )
    contrib = contrib.reshape(n_cols, n_blocks * 6)
    sub_index = lax.axis_index(("gx", "gy", "gz"))
    zone_count = ZONE_DEV * lax.axis_size(("gx", "gy", "gz"))
    relative = (zone_map.reshape(-1) - sub_index * ZONE_DEV) % zone_count
    window = (relative[:, None] == jnp.arange(2 * ZONE_DEV, dtype=jnp.int32)[None, :]).astype(
        jnp.float32
    )
    partial_sums = jnp.dot(contrib, window, precision=lax.Precision.HIGHEST)
    carried = passed_along(partial_sums[:, ZONE_DEV:], ("gx", "gy", "gz"), 1)
    sensitivity = partial_sums[:, :ZONE_DEV] + carried
    return (adjoint, sensitivity)


def solution(mesh):
    in_specs = (
        P(None, ("gx", "gy", "gz")),
        P(("gx", "gy", "gz")),
        P(("gx", "gy", "gz"), None, None),
        P(("gx", "gy", "gz"), None),
        P(("gx", "gy", "gz"), None),
        P(("gx", "gy", "gz"), None),
    )
    out_specs = (P(None, ("gx", "gy", "gz")), P(None, ("gx", "gy", "gz")))
    return jax.shard_map(
        on_device, mesh=mesh, in_specs=in_specs, out_specs=out_specs, check_vma=False
    )
```

profile of v0, /device:TPU:32, one launch (start us, length us, event | category | flops | bytes accessed | tf_op | source)
XLA Modules:
  0.0 454.5 jit_solution(14941745477132748042)
XLA Ops:
  0.6 11.1 %copy.20 = f32[64,7,4096]{0,2,1:T(8,128)} copy(f32[64,7,4096]{2,0,1:T(8,128)} %param.11) | data formatting | bytes 14680064 | tf_op args[2]
  11.7 3.2 slice_bitcast_fusion
  14.9 1.5 gather_fusion
  18.2 3.4 collective-permute-start
  21.7 3.3 collective-permute-start.1
  25.1 3.5 collective-permute-start.2
  28.7 1.3 collective-permute-start.3
  30.1 1.3 collective-permute-start.4
  31.5 16.3 %copy.24 = f32[64,7,64,64]{3,2,1,0:T(8,128)} copy(f32[64,7,64,64]{0,3,2,1:T(8,128)} %bitcast.102) | data formatting | bytes 14680064 | tf_op jit(solution)/shard_map/reshape | solution.py:51
  49.2 1.3 collective-permute-start.5
  50.6 5.0 %collective-permute-done.5 = f32[1,16,1024]{2,1,0:T(8,128)S(1)} collective-permute-done((f32[1,16,1024]{2,1,0:T(8,128)S(1)}, f32[1,16,1024]{2,1,0:T(8,128)S(1)}, u32[]{:S(2)}, u32[]{:S(2)}) %collective-permute-start.5) | collective-permute-done | bytes 65568 | tf_op jit(solution)/shard_map/ppermute | solution.py:20
  55.9 2.9 gather_fusion.2
  58.9 16.1 %convolution_bitcast_fusion.1 = f32[16,64,64]{2,0,1:T(8,128)S(1)} fusion(f32[64,7,16,64]{3,2,1,0:T(8,128)} %bitcast.106, f32[64,7,64,64]{3,2,1,0:T(8,128)} %copy.24), kind=kOutput, calls=%fused_computation.18 | convolution fusion | flops 352321536 | bytes 9437184 | tf_op jit(solution)/shard_map/akij,akcj->cai/dot_general | solution.py:83
  75.7 83.4 %all-reduce = (f32[16,16]{0,1:T(8,128)S(1)}, f32[16,16]{0,1:T(8,128)S(1)}) all-reduce(f32[16,16]{0,1:T(8,128)S(1)} %convolution_bitcast_fusion.2, f32[16,16]{0,1:T(8,128)S(1)} %fusion.12), channel_id=1, replica_groups=mesh['gx'=16,'gy'=4,'gz'=4] {'gx','gy','gz'}, use_global_device_ids=true, to_apply=%region_3.5 | all-reduce | flops 512 | bytes 4096 | tf_op jit(solution)/shard_map/psum | solution.py:43
  159.2 1.5 cholesky.70
  162.0 1.2 custom-call.12
  163.3 1.5 cholesky.59
  168.6 74.9 %psum.30 = f32[16,16]{1,0:T(8,128)S(1)} all-reduce(f32[16,16]{1,0:T(8,128)S(1)} %fusion.3), channel_id=1, replica_groups=mesh['gx'=16,'gy'=4,'gz'=4] {'gx','gy','gz'}, use_global_device_ids=true, to_apply=%region_4.7 | all-reduce | flops 256 | bytes 2048 | tf_op jit(solution)/shard_map/psum | solution.py:43
  245.7 3.3 collective-permute-start.6
  249.5 3.5 collective-permute-start.7
  253.0 3.2 collective-permute-start.8
  256.3 1.3 collective-permute-start.9
  257.7 1.3 collective-permute-start.10
  259.1 1.3 collective-permute-start.11
  260.5 2.0 collective-permute-done.9
  262.5 1.8 collective-permute-done.11
  264.7 2.9 gather_fusion.4
  267.6 16.1 %convolution_bitcast_fusion = f32[16,64,64]{2,0,1:T(8,128)S(1)} fusion(f32[64,7,16,64]{3,2,1,0:T(8,128)} %bitcast.105, f32[64,7,64,64]{3,2,1,0:T(8,128)} %copy.24), kind=kOutput, calls=%fused_computation.17 | convolution fusion | flops 352321536 | bytes 9437184 | tf_op jit(solution)/shard_map/akij,akcj->cai/dot_general | solution.py:83
  284.4 79.2 %psum.31 = f32[16,16]{0,1:T(8,128)S(1)} all-reduce(f32[16,16]{0,1:T(8,128)S(1)} %fusion.35), channel_id=1, replica_groups=mesh['gx'=16,'gy'=4,'gz'=4] {'gx','gy','gz'}, use_global_device_ids=true, to_apply=%region_5.8 | all-reduce | flops 256 | bytes 2048 | tf_op jit(solution)/shard_map/psum | solution.py:43
  363.8 1.5 cholesky.81
  370.8 3.6 collective-permute-start.12
  374.4 11.9 %slice.272 = f32[64,6,64,64]{0,3,2,1:T(8,128)} slice(f32[64,7,64,64]{0,3,2,1:T(8,128)} %bitcast.103), slice={[0:64], [1:7], [0:64], [0:64]} | slice | bytes 12582912 | tf_op jit(solution)/shard_map/slice | solution.py:108
  386.3 14.2 %copy.44 = f32[64,6,64,64]{2,3,1,0:T(8,128)} copy(f32[64,6,64,64]{0,3,2,1:T(8,128)} %slice.272) | data formatting | bytes 12582912 | tf_op jit(solution)/shard_map/slice | solution.py:108
  400.7 3.3 collective-permute-start.13
  404.1 3.3 collective-permute-start.14
  407.5 1.3 collective-permute-start.15
  408.9 1.3 collective-permute-start.16
  410.3 1.3 collective-permute-start.17
  411.7 2.1 collective-permute-done.15
  413.8 1.7 collective-permute-done.17
  415.5 1.3 reshape.109
  416.8 1.4 pad_maximum_fusion
  418.2 3.2 gather_fusion.6
  421.5 3.4 copy_subtract_fusion
  425.1 13.4 %fusion.7 = f32[64,6,1,64]{3,2,1,0:T(1,128)S(1)} fusion(f32[64,6,64,64]{2,3,1,0:T(8,128)} %copy.44, f32[64,6,64,1]{2,0,1,3:T(8,128)S(1)} %slice_bitcast_fusion.1), kind=kOutput, calls=%fused_computation.32 | convolution fusion | flops 18874368 | bytes 6488064 | tf_op jit(solution)/shard_map/akij,akj->aki/dot_general | solution.py:107
  438.5 7.3 %fusion = f32[64,6,1,16]{3,2,1,0:T(1,128)S(1)} fusion(f32[64,6,16,64]{3,0,2,1:T(8,128)S(1)} %slice.273, f32[64,6,64,1]{2,1,0,3:T(8,128)S(1)} %bitcast.111), kind=kOutput, calls=%fused_computation.11 | convolution fusion | flops 4718592 | bytes 1695744 | tf_op jit(solution)/shard_map/akci,aki->cak/dot_general | solution.py:110
  446.3 4.6 %collective-permute-start.18 = (f32[16,128]{1,0:T(8,128)S(1)}, f32[16,128]{1,0:T(8,128)S(1)}, u32[]{:S(2)}, u32[]{:S(2)}) collective-permute-start(f32[16,128]{1,0:T(8,128)S(1)} %slice.275), channel_id=1, source_target_pairs={{0,1},{1,2},{2,3},{3,4},{4,5},{5,6},{6,7},{7,8},{8,9},{9,10},{10,1... | collective-permute-start | bytes 24584 | tf_op jit(solution)/shard_map/ppermute | solution.py:30
  450.9 2.8 collective-permute-done.18
  (142 shorter events, 21.6 us)
Async XLA Ops:
  11.7 4.9 %copy-start = (f32[16,4096]{1,0:T(8,128)S(1)}, f32[16,4096]{1,0:T(8,128)}, u32[]{:S(2)}) copy-start(f32[16,4096]{1,0:T(8,128)} %param.9) | copy-start | bytes 786436
  11.7 5.4 %copy-start.4 = (s32[6,16]{1,0:T(8,128)S(1)}, s32[6,16]{1,0:T(8,128)}, u32[]{:S(2)}) copy-start(s32[6,16]{1,0:T(8,128)} %param.13) | copy-start | bytes 1156
  16.4 15.0 %copy-start.3 = (s32[64,7]{0,1:T(8,128)S(1)}, s32[64,7]{0,1:T(8,128)}, u32[]{:S(2)}) copy-start(s32[64,7]{0,1:T(8,128)} %param.12) | copy-start | bytes 5380
  18.2 31.0 %collective-permute-start = (f32[1,16,1024]{2,1,0:T(8,128)S(1)}, f32[1,16,1024]{2,1,0:T(8,128)S(1)}, u32[]{:S(2)}, u32[]{:S(2)}) collective-permute-start(f32[1,16,1024]{2,1,0:T(8,128)S(1)} %slice.179), channel_id=1, source_target_pairs={{0,16},{16,32},{32,48},{48,64},{64,80},{80,96},{96,112},{112,128},... | collective-permute-start | bytes 196616 | tf_op jit(solution)/shard_map/ppermute | solution.py:18
  21.7 28.9 %collective-permute-start.1 = (f32[1,16,1024]{2,1,0:T(8,128)S(1)}, f32[1,16,1024]{2,1,0:T(8,128)S(1)}, u32[]{:S(2)}, u32[]{:S(2)}) collective-permute-start(f32[1,16,1024]{2,1,0:T(8,128)S(1)} %slice.181), channel_id=1, source_target_pairs={{16,0},{32,16},{48,32},{64,48},{80,64},{96,80},{112,96},{128,112},... | collective-permute-start | bytes 196616 | tf_op jit(solution)/shard_map/ppermute | solution.py:20
  25.1 25.4 %collective-permute-start.2 = (f32[1,16,1024]{2,1,0:T(8,128)S(1)}, f32[1,16,1024]{2,1,0:T(8,128)S(1)}, u32[]{:S(2)}, u32[]{:S(2)}) collective-permute-start(f32[1,16,1024]{2,1,0:T(8,128)S(1)} %slice.183), channel_id=1, source_target_pairs={{0,4},{4,8},{8,12},{1,5},{5,9},{9,13},{2,6},{6,10},{10,14},{3,7},{... | collective-permute-start | bytes 196616 | tf_op jit(solution)/shard_map/ppermute | solution.py:18
  28.7 21.9 %collective-permute-start.3 = (f32[1,16,1024]{2,1,0:T(8,128)S(1)}, f32[1,16,1024]{2,1,0:T(8,128)S(1)}, u32[]{:S(2)}, u32[]{:S(2)}) collective-permute-start(f32[1,16,1024]{2,1,0:T(8,128)S(1)} %slice.185), channel_id=1, source_target_pairs={{4,0},{8,4},{12,8},{5,1},{9,5},{13,9},{6,2},{10,6},{14,10},{7,3},{... | collective-permute-start | bytes 196616 | tf_op jit(solution)/shard_map/ppermute | solution.py:20
  30.1 20.5 %collective-permute-start.4 = (f32[1,16,1024]{2,1,0:T(8,128)S(1)}, f32[1,16,1024]{2,1,0:T(8,128)S(1)}, u32[]{:S(2)}, u32[]{:S(2)}) collective-permute-start(f32[1,16,1024]{2,1,0:T(8,128)S(1)} %slice.187), channel_id=1, source_target_pairs={{0,1},{1,2},{2,3},{4,5},{5,6},{6,7},{8,9},{9,10},{10,11},{12,13},{... | collective-permute-start | bytes 196616 | tf_op jit(solution)/shard_map/ppermute | solution.py:18
  31.4 17.4 %copy-start.2 = (f32[4096]{0:T(1024)S(1)}, f32[4096]{0:T(1024)}, u32[]{:S(2)}) copy-start(f32[4096]{0:T(1024)} %param.10) | copy-start | bytes 49156
  31.5 17.5 %copy-start.5 = (s32[64,6]{0,1:T(8,128)S(1)}, s32[64,6]{0,1:T(8,128)}, u32[]{:S(2)}) copy-start(s32[64,6]{0,1:T(8,128)} %param.14) | copy-start | bytes 4612
  49.2 6.4 %collective-permute-start.5 = (f32[1,16,1024]{2,1,0:T(8,128)S(1)}, f32[1,16,1024]{2,1,0:T(8,128)S(1)}, u32[]{:S(2)}, u32[]{:S(2)}) collective-permute-start(f32[1,16,1024]{2,1,0:T(8,128)S(1)} %slice.189), channel_id=1, source_target_pairs={{1,0},{2,1},{3,2},{5,4},{6,5},{7,6},{9,8},{10,9},{11,10},{13,12},{... | collective-permute-start | bytes 196616 | tf_op jit(solution)/shard_map/ppermute | solution.py:20
  245.7 13.4 %collective-permute-start.6 = (f32[1,16,1024]{2,1,0:T(8,128)S(1)}, f32[1,16,1024]{2,1,0:T(8,128)S(1)}, u32[]{:S(2)}, u32[]{:S(2)}) collective-permute-start(f32[1,16,1024]{2,1,0:T(8,128)S(1)} %slice.191), channel_id=1, source_target_pairs={{0,16},{16,32},{32,48},{48,64},{64,80},{80,96},{96,112},{112,128},... | collective-permute-start | bytes 196616 | tf_op jit(solution)/shard_map/ppermute | solution.py:18
  249.5 11.0 %collective-permute-start.7 = (f32[1,16,1024]{2,1,0:T(8,128)S(1)}, f32[1,16,1024]{2,1,0:T(8,128)S(1)}, u32[]{:S(2)}, u32[]{:S(2)}) collective-permute-start(f32[1,16,1024]{2,1,0:T(8,128)S(1)} %slice.193), channel_id=1, source_target_pairs={{16,0},{32,16},{48,32},{64,48},{80,64},{96,80},{112,96},{128,112},... | collective-permute-start | bytes 196616 | tf_op jit(solution)/shard_map/ppermute | solution.py:20
  253.0 7.4 %collective-permute-start.8 = (f32[1,16,1024]{2,1,0:T(8,128)S(1)}, f32[1,16,1024]{2,1,0:T(8,128)S(1)}, u32[]{:S(2)}, u32[]{:S(2)}) collective-permute-start(f32[1,16,1024]{2,1,0:T(8,128)S(1)} %slice.195), channel_id=1, source_target_pairs={{0,4},{4,8},{8,12},{1,5},{5,9},{9,13},{2,6},{6,10},{10,14},{3,7},{... | collective-permute-start | bytes 196616 | tf_op jit(solution)/shard_map/ppermute | solution.py:18
  256.3 6.2 %collective-permute-start.9 = (f32[1,16,1024]{2,1,0:T(8,128)S(1)}, f32[1,16,1024]{2,1,0:T(8,128)S(1)}, u32[]{:S(2)}, u32[]{:S(2)}) collective-permute-start(f32[1,16,1024]{2,1,0:T(8,128)S(1)} %slice.197), channel_id=1, source_target_pairs={{4,0},{8,4},{12,8},{5,1},{9,5},{13,9},{6,2},{10,6},{14,10},{7,3},{... | collective-permute-start | bytes 196616 | tf_op jit(solution)/shard_map/ppermute | solution.py:20
  257.7 4.8 %collective-permute-start.10 = (f32[1,16,1024]{2,1,0:T(8,128)S(1)}, f32[1,16,1024]{2,1,0:T(8,128)S(1)}, u32[]{:S(2)}, u32[]{:S(2)}) collective-permute-start(f32[1,16,1024]{2,1,0:T(8,128)S(1)} %slice.199), channel_id=1, source_target_pairs={{0,1},{1,2},{2,3},{4,5},{5,6},{6,7},{8,9},{9,10},{10,11},{12,13},{... | collective-permute-start | bytes 196616 | tf_op jit(solution)/shard_map/ppermute | solution.py:18
  259.1 5.2 %collective-permute-start.11 = (f32[1,16,1024]{2,1,0:T(8,128)S(1)}, f32[1,16,1024]{2,1,0:T(8,128)S(1)}, u32[]{:S(2)}, u32[]{:S(2)}) collective-permute-start(f32[1,16,1024]{2,1,0:T(8,128)S(1)} %slice.201), channel_id=1, source_target_pairs={{1,0},{2,1},{3,2},{5,4},{6,5},{7,6},{9,8},{10,9},{11,10},{13,12},{... | collective-permute-start | bytes 196616 | tf_op jit(solution)/shard_map/ppermute | solution.py:20
  368.6 0.7 copy-start.1
  370.8 39.5 %collective-permute-start.12 = (f32[1,16,1088]{2,1,0:T(8,128)S(1)}, f32[1,16,1088]{2,1,0:T(8,128)S(1)}, u32[]{:S(2)}, u32[]{:S(2)}) collective-permute-start(f32[1,16,1088]{2,1,0:T(8,128)S(1)} %slice.203), channel_id=1, source_target_pairs={{0,16},{16,32},{32,48},{48,64},{64,80},{80,96},{96,112},{112,128},... | collective-permute-start | bytes 208904 | tf_op jit(solution)/shard_map/ppermute | solution.py:18
  400.7 10.9 %collective-permute-start.13 = (f32[1,16,1088]{2,1,0:T(8,128)S(1)}, f32[1,16,1088]{2,1,0:T(8,128)S(1)}, u32[]{:S(2)}, u32[]{:S(2)}) collective-permute-start(f32[1,16,1088]{2,1,0:T(8,128)S(1)} %slice.205), channel_id=1, source_target_pairs={{16,0},{32,16},{48,32},{64,48},{80,64},{96,80},{112,96},{128,112},... | collective-permute-start | bytes 208904 | tf_op jit(solution)/shard_map/ppermute | solution.py:20
  404.1 7.6 %collective-permute-start.14 = (f32[1,16,1088]{2,1,0:T(8,128)S(1)}, f32[1,16,1088]{2,1,0:T(8,128)S(1)}, u32[]{:S(2)}, u32[]{:S(2)}) collective-permute-start(f32[1,16,1088]{2,1,0:T(8,128)S(1)} %slice.207), channel_id=1, source_target_pairs={{0,4},{4,8},{8,12},{1,5},{5,9},{9,13},{2,6},{6,10},{10,14},{3,7},{... | collective-permute-start | bytes 208904 | tf_op jit(solution)/shard_map/ppermute | solution.py:18
  407.5 6.2 %collective-permute-start.15 = (f32[1,16,1088]{2,1,0:T(8,128)S(1)}, f32[1,16,1088]{2,1,0:T(8,128)S(1)}, u32[]{:S(2)}, u32[]{:S(2)}) collective-permute-start(f32[1,16,1088]{2,1,0:T(8,128)S(1)} %slice.209), channel_id=1, source_target_pairs={{4,0},{8,4},{12,8},{5,1},{9,5},{13,9},{6,2},{10,6},{14,10},{7,3},{... | collective-permute-start | bytes 208904 | tf_op jit(solution)/shard_map/ppermute | solution.py:20
  408.9 4.9 %collective-permute-start.16 = (f32[1,16,1088]{2,1,0:T(8,128)S(1)}, f32[1,16,1088]{2,1,0:T(8,128)S(1)}, u32[]{:S(2)}, u32[]{:S(2)}) collective-permute-start(f32[1,16,1088]{2,1,0:T(8,128)S(1)} %slice.211), channel_id=1, source_target_pairs={{0,1},{1,2},{2,3},{4,5},{5,6},{6,7},{8,9},{9,10},{10,11},{12,13},{... | collective-permute-start | bytes 208904 | tf_op jit(solution)/shard_map/ppermute | solution.py:18
  410.3 5.2 %collective-permute-start.17 = (f32[1,16,1088]{2,1,0:T(8,128)S(1)}, f32[1,16,1088]{2,1,0:T(8,128)S(1)}, u32[]{:S(2)}, u32[]{:S(2)}) collective-permute-start(f32[1,16,1088]{2,1,0:T(8,128)S(1)} %slice.213), channel_id=1, source_target_pairs={{1,0},{2,1},{3,2},{5,4},{6,5},{7,6},{9,8},{10,9},{11,10},{13,12},{... | collective-permute-start | bytes 208904 | tf_op jit(solution)/shard_map/ppermute | solution.py:20
  446.3 7.4 %collective-permute-start.18 = (f32[16,128]{1,0:T(8,128)S(1)}, f32[16,128]{1,0:T(8,128)S(1)}, u32[]{:S(2)}, u32[]{:S(2)}) collective-permute-start(f32[16,128]{1,0:T(8,128)S(1)} %slice.275), channel_id=1, source_target_pairs={{0,1},{1,2},{2,3},{3,4},{4,5},{5,6},{6,7},{7,8},{8,9},{9,10},{10,1... | collective-permute-start | bytes 24584 | tf_op jit(solution)/shard_map/ppermute | solution.py:30
where the time goes:
time: 463 us; the launch traced here: 454 us
  blocking collectives  238 us (51%)
  local copies, waits for them, and re-layouts  77.7 us (17%)
  matrix products  57.7 us (12%)
  starting transfers between devices  46.6 us (10%)
  other arithmetic  17.8 us (4%)
  waiting for transfers between devices  15.5 us (3%)
    psum x3, blocking collectives, total_gram(): return lax.psum(value, ('gx', 'gy', 'gz'))  238 us
    dot_general x2, matrix products, on_device(): jnp.einsum('akij,akcj->cai', blocks, gathered, precision=lax.Precision.HI...  32.1 us
    slice x2, local copies, waits for them, and re-layouts, on_device(): blocks[:, 1:]  26.1 us
    ppermute x9, starting transfers between devices, extended_2(): lax.ppermute(tail, axis, [(i, (i + 1) % count) for i in range(ends)])  24.1 us
    ppermute x9, starting transfers between devices, extended_2(): lax.ppermute(head, axis, [((i + 1) % count, i) for i in range(ends)])  17.9 us
    reshape x1, local copies, waits for them, and re-layouts, on_device(): blocks = stiffness.reshape(n_blocks, 7, block_dof, block_dof)  16.3 us
    dot_general x1, matrix products, on_device(): jnp.einsum('akij,akj->aki', blocks[:, 1:], differ[:, :, n_cols], precisio...  13.4 us
    ppermute x9, waiting for transfers between devices, extended_2(): lax.ppermute(head, axis, [((i + 1) % count, i) for i in range(ends)])  12.6 us
  transfers between devices with their start and end apart: 19, of which 6 were waited for; matrix products, arithmetic and copies ran while one was open for 10% of the time, Pallas kernels for 0%

commit v1 on v0

v1 whole, which is shorter than its diff:
```python
import functools

import jax
import jax.numpy as jnp
from jax import lax
from jax.experimental import pallas as pl
from jax.experimental.pallas import tpu as pltpu
from jax.sharding import PartitionSpec as P

MESH = pl.DeviceIdType.MESH
F32 = jnp.float32
BF16 = jnp.bfloat16
NODES = 64
DOF = 64
COLS = 16
LANES = 128
GROUPS = 16
EXT = 160
ZONE_DEV = 128
PAIRS = ((0, 2), (4, 6), (1, 3), (5, None))
FACE_ROWS = 8 * COLS + 8


def nt(a, b):
    return lax.dot_general(a, b, (((1,), (1,)), ((), ())), preferred_element_type=F32)


def nn(a, b):
    return lax.dot_general(a, b, (((1,), (0,)), ((), ())), preferred_element_type=F32)


def exact_nn(a, b):
    return lax.dot_general(
        a, b, (((1,), (0,)), ((), ())), preferred_element_type=F32, precision=lax.Precision.HIGHEST
    )


def exact_nt(a, b):
    return lax.dot_general(
        a, b, (((1,), (1,)), ((), ())), preferred_element_type=F32, precision=lax.Precision.HIGHEST
    )


def halves(x):
    high = x.astype(BF16)
    return high, (x - high.astype(F32)).astype(BF16)


def thirds(x):
    high = x.astype(BF16)
    rest = x - high.astype(F32)
    mid = rest.astype(BF16)
    return high, mid, (rest - mid.astype(F32)).astype(BF16)


def iota(shape, dim):
    return lax.broadcasted_iota(jnp.int32, shape, dim)


def lower(rows=COLS):
    return iota((rows, LANES), 1) < DOF


def kernel(
    sizes,
    loads_ref, disp_ref, stiff_ref, col_ref, face_ref, zone_ref,
    adj_ref, sens_ref,
    m_ref, wh_ref, wl_ref,
    zf, zh, zl, wf, wh0, wl0,
    zp_ref, qs_ref, qp_ref, wp_ref, vp_ref, xa_ref,
    dinv_ref, dpack_ref, dsplit_ref, dext_ref, dd_ref,
    mvh_ref, mvl_ref, oh_ref, term_ref,
    zsend, wsend, zrecv, wrecv,
    g1_ref, g2_ref, g1_slots, g2_slots, x1_ref, x2_ref, x1_slots, x2_slots,
    part_ref, carry_ref,
    load_sems, z_send_sems, z_recv_sems, w_send_sems, w_recv_sems,
    red_send_sems, red_recv_sems, carry_sems,
):
    nx, ny, nz = sizes
    nb = ny * nz
    mx, my, mz = lax.axis_index("gx"), lax.axis_index("gy"), lax.axis_index("gz")
    mb = my * nz + mz
    me = mx * nb + mb
    total = nx * nb

    def along(i):
        return (lax.rem(mx + i, nx), my, mz)

    def across(i):
        b = lax.rem(mb + i, nb)
        return (mx, b // nz, lax.rem(b, nz))

    def flat(i):
        s = lax.rem(me + i + total, total)
        b = lax.rem(s, nb)
        return (s // nb, b // nz, lax.rem(b, nz))

    barrier = pltpu.get_barrier_semaphore()
    for i in range(1, nx):
        pl.semaphore_signal(barrier, inc=1, device_id=along(i), device_id_type=MESH)
    for i in range(1, nb):
        pl.semaphore_signal(barrier, inc=1, device_id=across(i), device_id_type=MESH)
    pl.semaphore_signal(barrier, inc=1, device_id=flat(-1), device_id_type=MESH)

    rows_k = NODES // 8 * 32 * 8

    def stiff_copy(k):
        part = pl.ds(k * rows_k, rows_k)
        return pltpu.make_async_copy(stiff_ref.at[part], m_ref.at[part], load_sems.at[k])

    for pair in PAIRS:
        for k in pair:
            if k is not None:
                stiff_copy(k).start()

    lo16, lo8, lo32 = lower(), lower(8), lower(32)

    prow, pcol = iota((256, 256), 0), iota((256, 256), 1)
    perm = jnp.where(
        (prow // DOF == pcol // DOF)
        & ((prow % DOF) // 32 + 2 * (prow % 32) == pcol % DOF),
        1.0, 0.0,
    ).astype(BF16)

    def put_rows(base, count, packed):
        turned = pltpu.roll(packed, DOF, 1)
        low = lower(count)
        dext_ref[pl.ds(base, count, stride=2), :] = jnp.where(low, packed, turned)
        dext_ref[pl.ds(base + 1, count, stride=2), :] = jnp.where(low, turned, packed)

    put_rows(0, 32, disp_ref[...])

    rel = lax.rem(zone_ref[...] - me * ZONE_DEV + total * ZONE_DEV, total * ZONE_DEV).astype(F32)
    rel = jnp.concatenate([jnp.zeros((1, NODES), F32), rel, jnp.zeros((1, NODES), F32)], axis=0)
    spread = jnp.where(iota((NODES, 512), 1) // 8 == iota((NODES, 512), 0), 1.0, 0.0).astype(BF16)
    spots = nn(rel.astype(BF16), spread)
    mine = iota((8, 512), 1) % 8 == iota((8, 512), 0)
    spot = jnp.sum(jnp.where(mine, spots, 0.0), axis=0, keepdims=True)
    entry = iota((1, 512), 1) % 8
    spot = jnp.where((entry == 0) | (entry == 7), -1.0, spot)
    for part in range(0, 2 * ZONE_DEV, 32):
        zone = (iota((32, 512), 0) + part).astype(F32)
        oh_ref[part : part + 32, :] = jnp.where(zone == spot, 1.0, 0.0).astype(BF16)

    stiff_copy(0).wait()
    lane8 = iota((8, LANES), 1)
    key = jnp.where(lane8 < DOF, lane8, lane8 - DOF)
    own = (key % 2 == 0) == (lane8 < DOF)
    key = jnp.where(own, key // 2, -1)

    def take_diagonal(octet, _):
        base = pl.multiple_of(octet * 256, 256)
        got = jnp.zeros((8, LANES), F32)
        for t in range(32):
            got = got + jnp.where(key == t, m_ref[pl.ds(base + t * 8, 8), :], 0.0)
        both = jnp.where(own, got, pltpu.roll(got, DOF, 1))
        dinv_ref[pl.ds(pl.multiple_of(octet * 8, 8), 8), :] = 1.0 / both
        return 0

    lax.fori_loop(0, 8, take_diagonal, 0)
    dpack_ref[...] = jnp.where(
        lo32, dinv_ref[pl.ds(0, 32, stride=2), :], dinv_ref[pl.ds(1, 32, stride=2), :]
    )
    dhi, dmid, dlo = thirds(dpack_ref[...])
    small = perm[:LANES, :LANES]
    dsplit_ref[...] = nt(dhi, small) + nt(dmid, small) + nt(dlo, small)

    def put_nodes(tile, node, full, high, low):
        turned = pltpu.roll(tile, DOF, 1)
        for i, x in enumerate((jnp.where(lo16, tile, turned), jnp.where(lo16, turned, tile))):
            full[node + i] = x
            xh, xl = halves(x)
            high[node + i] = xh
            low[node + i] = xl

    def start_z(tau, _):
        lanes = pl.ds(pl.multiple_of(tau * LANES, LANES), LANES)
        tile = loads_ref[:, lanes] * dpack_ref[pl.ds(tau, 1), :]
        zp_ref[:, lanes] = tile
        put_nodes(tile, 2 * tau, zf, zh, zl)
        return 0

    lax.fori_loop(0, 32, start_z, 0, unroll=8)

    def fill_face(d, full, buf):
        for q in range(8):
            a, b = face_ref[d, 2 * q], face_ref[d, 2 * q + 1]
            buf[d, q * COLS : (q + 1) * COLS, :] = jnp.where(lo16, full[a], full[b])

    def fill_disp(d, buf):
        got = jnp.zeros((8, LANES), F32)
        sub = iota((8, LANES), 0)
        for q in range(8):
            a, b = face_ref[d, 2 * q], face_ref[d, 2 * q + 1]
            pair = jnp.where(lower(1), dext_ref[pl.ds(a, 1), :], dext_ref[pl.ds(b, 1), :])
            got = jnp.where(sub == q, jnp.broadcast_to(pair, (8, LANES)), got)
        buf[d, 8 * COLS : FACE_ROWS, :] = got

    place = (mx, mx, my, my, mz, mz)
    counts = (nx, nx, ny, ny, nz, nz)

    def has(d):
        return place[d] > 0 if d % 2 == 0 else place[d] < counts[d] - 1

    def neighbour(d):
        step = -1 if d % 2 == 0 else 1
        there = lax.rem(place[d] + step + counts[d], counts[d])
        return ((there, my, mz), (mx, there, mz), (mx, my, there))[d // 2]

    def face_copy(d, send, recv, send_sems, recv_sems):
        return pltpu.make_async_remote_copy(
            src_ref=send.at[d], dst_ref=recv.at[d ^ 1],
            send_sem=send_sems.at[d], recv_sem=recv_sems.at[d ^ 1],
            device_id=neighbour(d), device_id_type=MESH,
        )

    def face_arrival(d, send, recv, send_sems, recv_sems):
        return pltpu.make_async_remote_copy(
            src_ref=send.at[d], dst_ref=recv.at[d],
            send_sem=send_sems.at[d], recv_sem=recv_sems.at[d],
            device_id=neighbour(d), device_id_type=MESH,
        )

    zline = (zsend, zrecv, z_send_sems, z_recv_sems)
    wline = (wsend, wrecv, w_send_sems, w_recv_sems)

    for d in range(6):
        fill_face(d, zf, zsend)
        fill_disp(d, zsend)

    pl.semaphore_wait(barrier, nx - 1 + nb - 1 + 1)

    def send_face(d, line):
        @pl.when(has(d))
        def _():
            face_copy(d, *line).start()

    def await_face(d, line):
        @pl.when(has(d))
        def _():
            face_arrival(d, *line).wait_recv()

        @pl.when(jnp.logical_not(has(d)))
        def _():
            line[1][d] = jnp.zeros(line[1].shape[1:], F32)

    def end_face(d, line):
        @pl.when(has(d))
        def _():
            face_copy(d, *line).wait_send()

    for d in range(6):
        send_face(d, zline)

    for at, (first, second) in enumerate(PAIRS):
        for k in (first, second):
            if k:
                stiff_copy(k).wait()

        def relay(octet, _, first=first, second=second, at=at):
            for s in range(8):
                base = pl.multiple_of((first * 8 + octet) * 256, 256)
                a = m_ref[pl.ds(base + s, 32, stride=8), :]
                ar = pltpu.roll(a, DOF, 1)
                if second is None:
                    b = br = jnp.zeros((32, LANES), F32)
                else:
                    base = pl.multiple_of((second * 8 + octet) * 256, 256)
                    b = m_ref[pl.ds(base + s, 32, stride=8), :]
                    br = pltpu.roll(b, DOF, 1)
                for p, x in enumerate((jnp.where(lo32, a, br), jnp.where(lo32, ar, b))):
                    xh, xl = halves(x)
                    rows = pl.ds(pl.multiple_of(octet * 512, 512) + s * DOF + p * 32, 32)
                    wh_ref[rows, at * LANES : (at + 1) * LANES] = xh
                    wl_ref[rows, at * LANES : (at + 1) * LANES] = xl
            return 0

        lax.fori_loop(0, 8, relay, 0)

    def take_face(d, line, full, high, low):
        recv = line[1]
        for q in range(8):
            put_nodes(recv[d, q * COLS : (q + 1) * COLS, :], NODES + d * 16 + 2 * q, full, high, low)

    for d in range(6):
        await_face(d, zline)
    for d in range(6):
        take_face(d, zline, zf, zh, zl)
        put_rows(NODES + d * 16, 8, zrecv[d, 8 * COLS : FACE_ROWS, :])

    def gathered(group, source, tiles, scale=None):
        rows = []
        for r4 in range(4):
            r = group * 4 + r4
            parts = []
            for at in range(tiles):
                first, second = PAIRS[at]
                a = source[col_ref[first, r]]
                b = jnp.zeros_like(a) if second is None else source[col_ref[second, r]]
                x = jnp.where(lo16, a, b)
                parts.append(x * scale if scale is not None and at == 0 else x)
            rows.append(jnp.concatenate(parts, axis=1))
        return jnp.concatenate(rows, axis=0)

    def multiply(group, high, low, tiles):
        rows = pl.ds(pl.multiple_of(group * 256, 256), 256)
        depth = tiles * LANES
        n = high.shape[0]
        weights = wh_ref[rows, :depth]
        both = nt(jnp.concatenate([high, low], axis=0), weights)
        return both[:n] + both[n:] + nt(high, wl_ref[rows, :depth])

    def own_part(x):
        return jnp.concatenate(
            [
                jnp.where(lo16, x[0:16, :LANES], x[16:32, :LANES]),
                jnp.where(lo16, x[32:48, LANES:], x[48:64, LANES:]),
            ],
            axis=1,
        )

    def image(group, _):
        out = multiply(group, gathered(group, zh, 4), gathered(group, zl, 4), 4)
        qs_ref[pl.ds(pl.multiple_of(group * COLS, COLS), COLS), :] = own_part(out)
        return 0

    lax.fori_loop(0, GROUPS, image, 0, unroll=4)

    def natural(group, _):
        rows = pl.ds(pl.multiple_of(group * 64, 64), 64)
        hi, mid, lo = thirds(qs_ref[rows, :])
        out = nn(jnp.concatenate([hi, mid, lo], axis=0), perm)
        out = out[:64] + out[64:128] + out[128:]
        for i in range(4):
            for h in range(2):
                tau = group * 8 + i * 2 + h
                lanes = pl.ds(pl.multiple_of(tau * LANES, LANES), LANES)
                tile = out[i * COLS : (i + 1) * COLS, h * LANES : (h + 1) * LANES]
                qp_ref[:, lanes] = tile
                tile = tile * dpack_ref[pl.ds(tau, 1), :]
                wp_ref[:, lanes] = tile
                put_nodes(tile, 2 * tau, wf, wh0, wl0)
        return 0

    lax.fori_loop(0, 4, natural, 0, unroll=4)

    for d in (0, 2, 4, 1, 3, 5):
        fill_face(d, wf, wsend)
        send_face(d, wline)

    def gram(left, right):
        lh, ll = halves(left)
        rh, rl = halves(right)
        both = nt(jnp.concatenate([lh, ll], axis=0), rh)
        n = left.shape[0]
        return both[:n] + both[n:] + nt(lh, rl)

    def product(step, sums):
        lanes = pl.ds(pl.multiple_of(step * 512, 512), 512)
        z, q, w = zp_ref[:, lanes], qp_ref[:, lanes], wp_ref[:, lanes]
        n0 = gram(loads_ref[:, lanes], z)
        cw = gram(jnp.concatenate([z, w], axis=0), q)
        return sums[0] + n0, sums[1] + cw[:16], sums[2] + cw[16:]

    zero16 = jnp.zeros((COLS, COLS), F32)
    grams = lax.fori_loop(0, 8, product, (zero16, zero16, zero16), unroll=4)

    row16, lane16 = iota((COLS, LANES), 0), iota((COLS, LANES), 1)
    fits16 = row16 % 8 == lane16 // 16
    sub8 = iota((8, LANES), 0)
    fits8 = sub8 == lane8 // 16

    def repeated(x):
        x = jnp.concatenate([x, jnp.zeros((COLS, LANES - COLS), F32)], axis=1)
        for by in (16, 32, 64):
            x = x + pltpu.roll(x, by, 1)
        return x

    def flattened(x):
        x = jnp.where(fits16, repeated(x), 0.0)
        return [jnp.sum(x[0:8], axis=0, keepdims=True), jnp.sum(x[8:16], axis=0, keepdims=True)]

    def unflattened(rows):
        out = []
        for row in rows:
            x = jnp.where(fits8, jnp.broadcast_to(row, (8, LANES)), 0.0)
            for by in (16, 32, 64):
                x = x + pltpu.roll(x, by, 1)
            out.append(x)
        return jnp.concatenate(out, axis=0)

    def red_copy(i, stage, src, slots, peer):
        return pltpu.make_async_remote_copy(
            src_ref=src, dst_ref=slots.at[i - 1],
            send_sem=red_send_sems.at[stage], recv_sem=red_recv_sems.at[stage],
            device_id=peer(i), device_id_type=MESH,
        )

    def red_all(stage, slots, peer):
        return pltpu.make_async_remote_copy(
            src_ref=slots, dst_ref=slots,
            send_sem=red_send_sems.at[stage], recv_sem=red_recv_sems.at[stage],
            device_id=peer(1), device_id_type=MESH,
        )

    def red_send(stage, src, slots, peer, count):
        for i in range(1, count):
            red_copy(i, stage, src, slots, peer).start()

    def red_sum(stage, src, slots, peer):
        red_all(stage, slots, peer).wait_recv()
        got = [src[...]] + [slots[i] for i in range(slots.shape[0])]
        while len(got) > 1:
            got = [a + b for a, b in zip(got[::2], got[1::2])] + got[len(got) & ~1 :]
        return got[0]

    rows = flattened(grams[0]) + flattened(grams[1]) + flattened(grams[2])
    packed = jnp.zeros((8, LANES), F32)
    for i, row in enumerate(rows):
        packed = jnp.where(sub8 == i, jnp.broadcast_to(row, (8, LANES)), packed)
    g1_ref[...] = packed
    red_send(0, g1_ref, g1_slots, along, nx)

    def differ(r, _):
        got = jnp.zeros((8, LANES), F32)
        for k in range(1, 7):
            there = jnp.broadcast_to(dext_ref[pl.ds(col_ref[k, r], 1), :], (8, LANES))
            here = jnp.broadcast_to(dext_ref[pl.ds(r, 1), :], (8, LANES))
            got = jnp.where(sub8 == k, here - there, got)
        dd_ref[pl.ds(pl.multiple_of(r * 8, 8), 8), :] = got
        return 0

    lax.fori_loop(0, NODES, differ, 0, unroll=8)

    k32, lane32 = iota((32, LANES), 0) % 8, iota((32, LANES), 1)
    fit256 = iota((32, 256), 0) // 8 == iota((32, 256), 1) // DOF

    def moved(group, _):
        rows = pl.ds(pl.multiple_of(group * 32, 32), 32)
        d = dd_ref[rows, :]
        parts = []
        for first, second in PAIRS:
            keep = (k32 == first) & (lane32 < DOF)
            if second is not None:
                keep = keep | ((k32 == second) & (lane32 >= DOF))
            parts.append(jnp.where(keep, d, 0.0))
        hi, lo = halves(jnp.concatenate(parts, axis=1))
        out = jnp.where(fit256, multiply(group, hi, lo, 4), 0.0)
        hi, lo = halves(out)
        out = nn(jnp.concatenate([hi, lo], axis=0), perm)
        mvh_ref[rows, :] = out[:32].astype(BF16)
        mvl_ref[rows, :] = out[32:].astype(BF16)
        return 0

    lax.fori_loop(0, GROUPS, moved, 0, unroll=4)

    g2_ref[...] = red_sum(0, g1_ref, g1_slots, along)
    red_send(1, g2_ref, g2_slots, across, nb)

    for d in (1, 3, 5):
        await_face(d, wline)
    for d in (1, 3, 5):
        take_face(d, wline, wf, wh0, wl0)

    half = jnp.where(lo16, 0.5, 1.0).astype(BF16)

    def curve(group, total_):
        out = multiply(group, gathered(group, wh0, 2, half), gathered(group, wl0, 2, half), 2)
        y = own_part(out)
        w = qs_ref[pl.ds(pl.multiple_of(group * COLS, COLS), COLS), :]
        w = w * jnp.concatenate(
            [dsplit_ref[pl.ds(group * 2, 1), :], dsplit_ref[pl.ds(group * 2 + 1, 1), :]], axis=1
        )
        yh, yl = halves(y)
        wh_, wl_ = halves(w)
        a = nt(jnp.concatenate([wh_, wl_], axis=0), yh)
        b = nt(jnp.concatenate([yh, yl], axis=0), wh_)
        return total_ + a[:16] + a[16:] + b[:16] + b[16:] + nt(wh_, yl) + nt(yh, wl_)

    curved = lax.fori_loop(0, GROUPS, curve, zero16, unroll=4)
    x1_ref[...] = jnp.concatenate(flattened(curved), axis=0)
    red_send(2, x1_ref, x1_slots, along, nx)

    kinds = [(iota((COLS, LANES), 1) // 32, iota((COLS, LANES), 1) % 8)]

    def terms(four, base, full):
        rows = pl.ds(pl.multiple_of(four * LANES, LANES), LANES)
        mh, ml = mvh_ref[rows, :], mvl_ref[rows, :]
        got = jnp.zeros((COLS, LANES), F32)
        for g in range(4):
            r = (four * 4 + g) * 4
            here = [jnp.where(lo16, full[r + 2 * h], full[r + 2 * h + 1]) for h in range(2)]
            parts = []
            for k in range(1, 7):
                parts.append(
                    jnp.concatenate(
                        [
                            here[h]
                            - jnp.where(
                                lo16, full[col_ref[k, r + 2 * h]], full[col_ref[k, r + 2 * h + 1]]
                            )
                            for h in range(2)
                        ],
                        axis=1,
                    )
                )
            hi, lo = halves(jnp.concatenate(parts, axis=0))
            both = nt(jnp.concatenate([hi, lo], axis=0), mh)
            out = both[:96] + both[96:] + nt(hi, ml)
            for k in range(1, 7):
                keep = (kinds[0][0] == g) & (kinds[0][1] == k)
                got = got + jnp.where(keep, out[(k - 1) * COLS : k * COLS], 0.0)
        term_ref[base : base + COLS, pl.ds(pl.multiple_of(four * LANES, LANES), LANES)] = 0.5 * got

    def terms_z(four, _):
        terms(four, 0, zf)
        return 0

    def terms_w(four, _):
        terms(four, COLS, wf)
        return 0

    lax.fori_loop(0, 4, terms_z, 0)

    x2_ref[...] = red_sum(2, x1_ref, x1_slots, along)
    red_send(3, x2_ref, x2_slots, across, nb)

    for d in (0, 2, 4):
        await_face(d, wline)
    for d in (0, 2, 4):
        take_face(d, wline, wf, wh0, wl0)
    lax.fori_loop(0, 4, terms_w, 0)

    hi, mid, lo = thirds(term_ref[...])
    sums = nt(jnp.concatenate([hi, mid, lo], axis=0), oh_ref[...])
    sums = sums[:32] + sums[32:64] + sums[64:]
    own_sums = sums[:, :ZONE_DEV]
    part_ref[...] = sums[:, ZONE_DEV:]
    carry = pltpu.make_async_remote_copy(
        src_ref=part_ref, dst_ref=carry_ref, send_sem=carry_sems.at[0], recv_sem=carry_sems.at[1],
        device_id=flat(1), device_id_type=MESH,
    )
    carry.start()

    def solved(x):
        n = x.shape[0]
        lane = iota((1, LANES), 1) % COLS
        for k in range(COLS):
            inv = 1.0 / x[k : k + 1, k : k + 1]
            column = jnp.broadcast_to(x[:, k : k + 1], (n, LANES)) * inv
            x = jnp.where(lane == k, column, x - column * jnp.broadcast_to(x[k : k + 1, :], (n, LANES)))
        return x[COLS:]

    g = red_sum(1, g2_ref, g2_slots, across)
    n0 = unflattened([g[0:1], g[1:2]])
    c0 = unflattened([g[2:3], g[3:4]])
    w0 = unflattened([g[4:5], g[5:6]])
    first = solved(jnp.concatenate([c0, n0, w0], axis=0))
    step0, mix = first[:COLS], first[COLS:]
    low16 = lane16 < COLS
    step0_, mix_ = jnp.where(low16, step0, 0.0), jnp.where(low16, mix, 0.0)

    pad = jnp.zeros((LANES - COLS, LANES), F32)

    def times(a, b):
        return exact_nn(a, jnp.concatenate([b, pad], axis=0))

    mix_w = times(mix_, w0)
    right = times(step0_, w0) - c0

    both = jnp.concatenate([step0[:, :COLS], mix[:, :COLS]], axis=0)
    bh, bm, bl = thirds(both)
    lhs = jnp.concatenate([bh, bh, bm, bh, bm, bl], axis=1)

    def prepare(step, _):
        lanes = pl.ds(pl.multiple_of(step * 512, 512), 512)
        ah, am, al = thirds(zp_ref[:, lanes])
        out = nn(lhs, jnp.concatenate([ah, am, ah, al, am, ah], axis=0))
        xa_ref[:, lanes] = out[:16]
        ah, am, al = thirds(out[16:] - wp_ref[:, lanes])
        vp_ref[0:16, lanes] = ah
        vp_ref[16:32, lanes] = am
        vp_ref[32:48, lanes] = al
        return 0

    lax.fori_loop(0, 8, prepare, 0, unroll=2)

    carry.wait_recv()
    all_sums = own_sums + carry_ref[...]
    ah, am, al = thirds(all_sums[:16])
    out = nn(lhs, jnp.concatenate([ah, am, ah, al, am, ah], axis=0))
    sens_a = out[:16]
    sens_v = thirds(out[16:] - all_sums[16:])

    x = red_sum(3, x2_ref, x2_slots, across)
    x = unflattened([x[0:1], x[1:2]])
    y = solved(jnp.concatenate([x - mix_w, right], axis=0))[:, :COLS]
    yh, ym, yl = thirds(y)
    lhs = jnp.concatenate([yh, yh, ym, yh, ym, yl], axis=1)

    def finish(step, _):
        lanes = pl.ds(pl.multiple_of(step * 512, 512), 512)
        v = vp_ref[:, lanes]
        ah, am, al = v[0:16], v[16:32], v[32:48]
        out = nn(lhs, jnp.concatenate([ah, am, ah, al, am, ah], axis=0))
        adj_ref[:, lanes] = xa_ref[:, lanes] + out
        return 0

    lax.fori_loop(0, 8, finish, 0, unroll=4)
    ah, am, al = sens_v
    sens_ref[...] = sens_a + nn(lhs, jnp.concatenate([ah, am, ah, al, am, ah], axis=0))

    for d in range(6):
        end_face(d, zline)
        end_face(d, wline)
    red_all(0, g1_slots, along).wait_send()
    red_all(1, g2_slots, across).wait_send()
    red_all(2, x1_slots, along).wait_send()
    red_all(3, x2_slots, across).wait_send()
    carry.wait_send()


def on_device(sizes, loads, displacement, stiffness, col_index, face_index, zone_map):
    nx, ny, nz = sizes
    nb = ny * nz
    tiles = jnp.transpose(stiffness, (1, 0, 2)).reshape(7, 8, 8, 32, LANES)
    tiles = jnp.transpose(tiles, (0, 1, 3, 2, 4)).reshape(7 * 8 * 32 * 8, LANES)
    vmem = pl.BlockSpec(memory_space=pltpu.VMEM)
    smem = pl.BlockSpec(memory_space=pltpu.SMEM)
    dma = pltpu.SemaphoreType.DMA
    v = pltpu.VMEM
    return pl.pallas_call(
        functools.partial(kernel, sizes),
        out_shape=(
            jax.ShapeDtypeStruct((COLS, NODES * DOF), F32),
            jax.ShapeDtypeStruct((COLS, ZONE_DEV), F32),
        ),
        in_specs=[vmem, vmem, pl.BlockSpec(memory_space=pl.ANY), smem, smem, vmem],
        out_specs=(vmem, vmem),
        scratch_shapes=[
            v((7 * 8 * 32 * 8, LANES), F32),
            v((NODES * DOF, 512), BF16), v((NODES * DOF, 512), BF16),
            v((EXT, COLS, LANES), F32), v((EXT, COLS, LANES), BF16), v((EXT, COLS, LANES), BF16),
            v((EXT, COLS, LANES), F32), v((EXT, COLS, LANES), BF16), v((EXT, COLS, LANES), BF16),
            v((COLS, NODES * DOF), F32), v((GROUPS * COLS, 256), F32),
            v((COLS, NODES * DOF), F32), v((COLS, NODES * DOF), F32),
            v((3 * COLS, NODES * DOF), BF16), v((COLS, NODES * DOF), F32),
            v((NODES, LANES), F32), v((32, LANES), F32), v((32, LANES), F32),
            v((EXT, LANES), F32), v((NODES * 8, LANES), F32),
            v((NODES * 8, 256), BF16), v((NODES * 8, 256), BF16),
            v((2 * ZONE_DEV, 512), BF16), v((2 * COLS, 512), F32),
            v((6, FACE_ROWS, LANES), F32), v((6, 8 * COLS, LANES), F32),
            v((6, FACE_ROWS, LANES), F32), v((6, 8 * COLS, LANES), F32),
            v((8, LANES), F32), v((8, LANES), F32),
            v((nx - 1, 8, LANES), F32), v((nb - 1, 8, LANES), F32),
            v((2, LANES), F32), v((2, LANES), F32),
            v((nx - 1, 2, LANES), F32), v((nb - 1, 2, LANES), F32),
            v((2 * COLS, ZONE_DEV), F32), v((2 * COLS, ZONE_DEV), F32),
            dma((7,)), dma((6,)), dma((6,)), dma((6,)), dma((6,)),
            dma((4,)), dma((4,)), dma((2,)),
        ],
        compiler_params=pltpu.CompilerParams(
            collective_id=0, has_side_effects=True, vmem_limit_bytes=48 * 1024 * 1024
        ),
        cost_estimate=pl.CostEstimate(
            flops=400_000_000, bytes_accessed=8_000_000, transcendentals=0
        ),
    )(
        loads, displacement.reshape(32, LANES), tiles,
        jnp.transpose(col_index), face_index, jnp.transpose(zone_map),
    )


def solution(mesh):
    sizes = (mesh.shape["gx"], mesh.shape["gy"], mesh.shape["gz"])
    axes = ("gx", "gy", "gz")
    in_specs = (
        P(None, axes), P(axes), P(axes, None, None), P(axes, None), P(axes, None), P(axes, None),
    )
    return jax.shard_map(
        functools.partial(on_device, sizes), mesh=mesh, in_specs=in_specs,
        out_specs=(P(None, axes), P(None, axes)), check_vma=False,
    )
```

time: 463 us -> 53.5 us (0.12)
  the two profiles are of different devices: /device:TPU:32 before, /device:TPU:1 now
where the time goes in v1:
time: 53.5 us; the launch traced here: 53.2 us
  Pallas kernels  47.5 us (89%)
  local copies, waits for them, and re-layouts  5.02 us (9%)
  between operations  0.65 us (1%)
    pallas_call x1, Pallas kernels, on_device(): pl.pallas_call(functools.partial(kernel, sizes), out_shape=(jax.ShapeDtyp...  47.5 us
    unnamed x12, local copies, waits for them, and re-layouts  5.02 us

profile of v1, /device:TPU:1, one launch (start us, length us, event | category | flops | bytes accessed | tf_op | source)
XLA Modules:
  0.0 53.2 jit_solution(10355986670641350309)
XLA Ops:
  0.6 0.0 copy-start
  0.6 0.9 %copy-done = f32[16,4096]{1,0:T(8,128)S(1)} copy-done((f32[16,4096]{1,0:T(8,128)S(1)}, f32[16,4096]{1,0:T(8,128)}, u32[]{:S(2)}) %copy-start) | copy-done | bytes 262168
  1.6 0.0 copy-start.1
  1.6 0.7 %copy-done.1 = f32[4096]{0:T(1024)S(1)} copy-done((f32[4096]{0:T(1024)S(1)}, f32[4096]{0:T(1024)}, u32[]{:S(2)}) %copy-start.1) | copy-done | bytes 16408
  2.3 0.0 copy-start.2
  2.3 0.7 %copy-done.2 = s32[64,7]{0,1:T(8,128)S(1)} copy-done((s32[64,7]{0,1:T(8,128)S(1)}, s32[64,7]{0,1:T(8,128)}, u32[]{:S(2)}) %copy-start.2) | copy-done | bytes 1816
  3.0 0.0 copy-start.3
  3.0 0.7 %copy-done.3 = s32[6,16]{1,0:T(8,128)S(1)} copy-done((s32[6,16]{1,0:T(8,128)S(1)}, s32[6,16]{1,0:T(8,128)}, u32[]{:S(2)}) %copy-start.3) | copy-done | bytes 408
  3.7 0.0 copy-start.4
  3.7 0.7 %copy-done.4 = s32[64,6]{0,1:T(8,128)S(1)} copy-done((s32[64,6]{0,1:T(8,128)S(1)}, s32[64,6]{0,1:T(8,128)}, u32[]{:S(2)}) %copy-start.4) | copy-done | bytes 1560
  4.4 47.5 %shard_map.77 = (f32[16,4096]{1,0:T(8,128)S(1)}, f32[16,128]{1,0:T(8,128)S(1)}) custom-call(f32[16,4096]{1,0:T(8,128)S(1)} %copy-done, f32[32,128]{1,0:T(8,128)S(1)} %bitcast.10, f32[14336,128]{1,0:T(8,128)} %bitcast.13, s32[7,64]{1,0:T(8,128)S(1)} %bitcast.11, s32[6,16]{1,0:T(8,128)S(1)} %copy-done.3, s32[6,64]{1,0:T(8,128)S(1)} %bitcast.12), custom_call_target="tpu_custom_call" | custom-call | flops 400000000 | bytes 8000000 | tf_op jit(solution)/shard_map/pallas_call | solution.py:632
  51.9 0.7 %copy.10 = f32[16,4096]{1,0:T(8,128)} copy(f32[16,4096]{1,0:T(8,128)S(1)} %get-tuple-element.4) | data formatting | bytes 524288
  52.6 0.6 %copy.11 = f32[16,128]{1,0:T(8,128)} copy(f32[16,128]{1,0:T(8,128)S(1)} %get-tuple-element.5) | data formatting | bytes 16384
Async XLA Ops:
  0.6 1.0 %copy-start = (f32[16,4096]{1,0:T(8,128)S(1)}, f32[16,4096]{1,0:T(8,128)}, u32[]{:S(2)}) copy-start(f32[16,4096]{1,0:T(8,128)} %loads_ref.1) | copy-start | bytes 786436
  1.6 0.7 %copy-start.1 = (f32[4096]{0:T(1024)S(1)}, f32[4096]{0:T(1024)}, u32[]{:S(2)}) copy-start(f32[4096]{0:T(1024)} %param.7) | copy-start | bytes 49156
  2.3 0.7 %copy-start.2 = (s32[64,7]{0,1:T(8,128)S(1)}, s32[64,7]{0,1:T(8,128)}, u32[]{:S(2)}) copy-start(s32[64,7]{0,1:T(8,128)} %param.9) | copy-start | bytes 5380
  3.0 0.7 %copy-start.3 = (s32[6,16]{1,0:T(8,128)S(1)}, s32[6,16]{1,0:T(8,128)}, u32[]{:S(2)}) copy-start(s32[6,16]{1,0:T(8,128)} %face_ref.1) | copy-start | bytes 1156
  3.7 0.7 %copy-start.4 = (s32[64,6]{0,1:T(8,128)S(1)}, s32[64,6]{0,1:T(8,128)}, u32[]{:S(2)}) copy-start(s32[64,6]{0,1:T(8,128)} %param.11) | copy-start | bytes 4612

commit v2 on v1

--- a/solution.py
+++ b/solution.py
@@ -63,17 +63,18 @@
 
 def kernel(
     sizes,
-    loads_ref, disp_ref, stiff_ref, col_ref, face_ref, zone_ref,
+    loads_in, disp_in, stiff_ref, col_in, face_in, zone_in,
     adj_ref, sens_ref,
-    m_ref, wh_ref, wl_ref,
+    loads_ref, disp_ref, col_ref, face_ref, zone_ref,
+    m_ref, w_ref,
     zf, zh, zl, wf, wh0, wl0,
     zp_ref, qs_ref, qp_ref, wp_ref, vp_ref, xa_ref,
     dinv_ref, dpack_ref, dsplit_ref, dext_ref, dd_ref,
-    mvh_ref, mvl_ref, oh_ref, term_ref,
+    mm_ref, mv_ref, pushed_ref, out_ref, oh_ref, term_ref, perm_ref,
     zsend, wsend, zrecv, wrecv,
     g1_ref, g2_ref, g1_slots, g2_slots, x1_ref, x2_ref, x1_slots, x2_slots,
     part_ref, carry_ref,
-    load_sems, z_send_sems, z_recv_sems, w_send_sems, w_recv_sems,
+    load_sems, input_sems, z_send_sems, z_recv_sems, w_send_sems, w_recv_sems,
     red_send_sems, red_recv_sems, carry_sems,
 ):
     nx, ny, nz = sizes
@@ -108,19 +109,32 @@
         part = pl.ds(k * rows_k, rows_k)
         return pltpu.make_async_copy(stiff_ref.at[part], m_ref.at[part], load_sems.at[k])
 
+    inputs = [
+        pltpu.make_async_copy(a, b, input_sems.at[i])
+        for i, (a, b) in enumerate((
+            (loads_in, loads_ref), (disp_in, disp_ref), (face_in, face_ref), (zone_in, zone_ref),
+            (col_in, col_ref),
+        ))
+    ]
+    stiff_copy(0).start()
+    for copy in inputs:
+        copy.start()
     for pair in PAIRS:
         for k in pair:
-            if k is not None:
+            if k:
                 stiff_copy(k).start()
 
     lo16, lo8, lo32 = lower(), lower(8), lower(32)
 
     prow, pcol = iota((256, 256), 0), iota((256, 256), 1)
-    perm = jnp.where(
+    perm_ref[...] = jnp.where(
         (prow // DOF == pcol // DOF)
         & ((prow % DOF) // 32 + 2 * (prow % 32) == pcol % DOF),
         1.0, 0.0,
     ).astype(BF16)
+
+    wh0[NODES:] = jnp.zeros((EXT - NODES, COLS, LANES), BF16)
+    wl0[NODES:] = jnp.zeros((EXT - NODES, COLS, LANES), BF16)
 
     def put_rows(base, count, packed):
         turned = pltpu.roll(packed, DOF, 1)
@@ -128,8 +142,10 @@
         dext_ref[pl.ds(base, count, stride=2), :] = jnp.where(low, packed, turned)
         dext_ref[pl.ds(base + 1, count, stride=2), :] = jnp.where(low, turned, packed)
 
+    inputs[1].wait()
     put_rows(0, 32, disp_ref[...])
 
+    inputs[3].wait()
     rel = lax.rem(zone_ref[...] - me * ZONE_DEV + total * ZONE_DEV, total * ZONE_DEV).astype(F32)
     rel = jnp.concatenate([jnp.zeros((1, NODES), F32), rel, jnp.zeros((1, NODES), F32)], axis=0)
     spread = jnp.where(iota((NODES, 512), 1) // 8 == iota((NODES, 512), 0), 1.0, 0.0).astype(BF16)
@@ -148,21 +164,25 @@
     own = (key % 2 == 0) == (lane8 < DOF)
     key = jnp.where(own, key // 2, -1)
 
-    def take_diagonal(octet, _):
-        base = pl.multiple_of(octet * 256, 256)
-        got = jnp.zeros((8, LANES), F32)
+    def take_diagonal(quarter, _):
+        got = [jnp.zeros((8, LANES), F32)] * 4
         for t in range(32):
-            got = got + jnp.where(key == t, m_ref[pl.ds(base + t * 8, 8), :], 0.0)
-        both = jnp.where(own, got, pltpu.roll(got, DOF, 1))
-        dinv_ref[pl.ds(pl.multiple_of(octet * 8, 8), 8), :] = 1.0 / both
-        return 0
-
-    lax.fori_loop(0, 8, take_diagonal, 0)
+            hit = key == t
+            for i in range(4):
+                base = pl.multiple_of(quarter * 1024, 1024)
+                got[i] = jnp.where(hit, m_ref[pl.ds(base + i * 256 + t * 8, 8), :], got[i])
+        for i in range(4):
+            both = jnp.where(own, got[i], pltpu.roll(got[i], DOF, 1))
+            rows = pl.ds(pl.multiple_of(quarter * 32, 32) + i * 8, 8)
+            dinv_ref[rows, :] = 1.0 / both
+        return 0
+
+    lax.fori_loop(0, 2, take_diagonal, 0)
     dpack_ref[...] = jnp.where(
         lo32, dinv_ref[pl.ds(0, 32, stride=2), :], dinv_ref[pl.ds(1, 32, stride=2), :]
     )
     dhi, dmid, dlo = thirds(dpack_ref[...])
-    small = perm[:LANES, :LANES]
+    small = perm_ref[:LANES, :LANES]
     dsplit_ref[...] = nt(dhi, small) + nt(dmid, small) + nt(dlo, small)
 
     def put_nodes(tile, node, full, high, low):
@@ -173,6 +193,11 @@
             high[node + i] = xh
             low[node + i] = xl
 
+    def put_full(tile, node, full):
+        turned = pltpu.roll(tile, DOF, 1)
+        full[node] = jnp.where(lo16, tile, turned)
+        full[node + 1] = jnp.where(lo16, turned, tile)
+
     def start_z(tau, _):
         lanes = pl.ds(pl.multiple_of(tau * LANES, LANES), LANES)
         tile = loads_ref[:, lanes] * dpack_ref[pl.ds(tau, 1), :]
@@ -180,7 +205,8 @@
         put_nodes(tile, 2 * tau, zf, zh, zl)
         return 0
 
-    lax.fori_loop(0, 32, start_z, 0, unroll=8)
+    inputs[0].wait()
+    lax.fori_loop(0, 32, start_z, 0, unroll=32)
 
     def fill_face(d, full, buf):
         for q in range(8):
@@ -224,6 +250,7 @@
     zline = (zsend, zrecv, z_send_sems, z_recv_sems)
     wline = (wsend, wrecv, w_send_sems, w_recv_sems)
 
+    inputs[2].wait()
     for d in range(6):
         fill_face(d, zf, zsend)
         fill_disp(d, zsend)
@@ -261,54 +288,44 @@
             for s in range(8):
                 base = pl.multiple_of((first * 8 + octet) * 256, 256)
                 a = m_ref[pl.ds(base + s, 32, stride=8), :]
-                ar = pltpu.roll(a, DOF, 1)
                 if second is None:
-                    b = br = jnp.zeros((32, LANES), F32)
+                    b = jnp.zeros((32, LANES), F32)
                 else:
                     base = pl.multiple_of((second * 8 + octet) * 256, 256)
                     b = m_ref[pl.ds(base + s, 32, stride=8), :]
-                    br = pltpu.roll(b, DOF, 1)
-                for p, x in enumerate((jnp.where(lo32, a, br), jnp.where(lo32, ar, b))):
+                turned = pltpu.roll(jnp.where(lo32, b, a), DOF, 1)
+                for p, x in enumerate((jnp.where(lo32, a, turned), jnp.where(lo32, turned, b))):
                     xh, xl = halves(x)
-                    rows = pl.ds(pl.multiple_of(octet * 512, 512) + s * DOF + p * 32, 32)
-                    wh_ref[rows, at * LANES : (at + 1) * LANES] = xh
-                    wl_ref[rows, at * LANES : (at + 1) * LANES] = xl
+                    row = pl.multiple_of(octet * 1024, 1024) + (s // 4) * 512 + (s % 4) * DOF + p * 32
+                    w_ref[pl.ds(row, 32), at * LANES : (at + 1) * LANES] = xh
+                    w_ref[pl.ds(row + 256, 32), at * LANES : (at + 1) * LANES] = xl
             return 0
 
-        lax.fori_loop(0, 8, relay, 0)
+        lax.fori_loop(0, 8, relay, 0, unroll=8)
 
     def take_face(d, line, full, high, low):
         recv = line[1]
         for q in range(8):
             put_nodes(recv[d, q * COLS : (q + 1) * COLS, :], NODES + d * 16 + 2 * q, full, high, low)
 
+    inputs[4].wait()
     for d in range(6):
         await_face(d, zline)
     for d in range(6):
         take_face(d, zline, zf, zh, zl)
         put_rows(NODES + d * 16, 8, zrecv[d, 8 * COLS : FACE_ROWS, :])
 
-    def gathered(group, source, tiles, scale=None):
+    def gathered(group, source):
         rows = []
         for r4 in range(4):
             r = group * 4 + r4
             parts = []
-            for at in range(tiles):
-                first, second = PAIRS[at]
+            for first, second in PAIRS:
                 a = source[col_ref[first, r]]
                 b = jnp.zeros_like(a) if second is None else source[col_ref[second, r]]
-                x = jnp.where(lo16, a, b)
-                parts.append(x * scale if scale is not None and at == 0 else x)
+                parts.append(jnp.where(lo16, a, b))
             rows.append(jnp.concatenate(parts, axis=1))
         return jnp.concatenate(rows, axis=0)
-
-    def multiply(group, high, low, tiles):
-        rows = pl.ds(pl.multiple_of(group * 256, 256), 256)
-        depth = tiles * LANES
-        n = high.shape[0]
-        weights = wh_ref[rows, :depth]
-        both = nt(jnp.concatenate([high, low], axis=0), weights)
-        return both[:n] + both[n:] + nt(high, wl_ref[rows, :depth])
 
     def own_part(x):
         return jnp.concatenate(
@@ -319,17 +336,48 @@
             axis=1,
         )
 
+    sub8 = iota((8, LANES), 0)
+    def differ(r, _):
+        got = jnp.zeros((8, LANES), F32)
+        for k in range(1, 7):
+            there = jnp.broadcast_to(dext_ref[pl.ds(col_ref[k, r], 1), :], (8, LANES))
+            here = jnp.broadcast_to(dext_ref[pl.ds(r, 1), :], (8, LANES))
+            got = jnp.where(sub8 == k, here - there, got)
+        dd_ref[pl.ds(pl.multiple_of(r * 8, 8), 8), :] = got
+        return 0
+
+    lax.fori_loop(0, NODES, differ, 0, unroll=16)
+
+    k32, lane32 = iota((32, LANES), 0) % 8, iota((32, LANES), 1)
+    fit256 = iota((32, 256), 0) // 8 == iota((32, 256), 1) // DOF
+
     def image(group, _):
-        out = multiply(group, gathered(group, zh, 4), gathered(group, zl, 4), 4)
+        small = pl.ds(pl.multiple_of(group * 32, 32), 32)
+        d = dd_ref[small, :]
+        parts = []
+        for first, second in PAIRS:
+            keep = (k32 == first) & (lane32 < DOF)
+            if second is not None:
+                keep = keep | ((k32 == second) & (lane32 >= DOF))
+            parts.append(jnp.where(keep, d, 0.0))
+        hi, lo = halves(jnp.concatenate(parts, axis=1))
+        rows = pl.ds(pl.multiple_of(group * 512, 512), 512)
+        left = jnp.concatenate([gathered(group, zh), hi, gathered(group, zl), lo], axis=0)
+        out = nt(left, w_ref[rows, :])
+        out = out[:96, :256] + (out[96:, :256] + (out[:96, 256:] + out[96:, 256:]))
         qs_ref[pl.ds(pl.multiple_of(group * COLS, COLS), COLS), :] = own_part(out)
-        return 0
-
-    lax.fori_loop(0, GROUPS, image, 0, unroll=4)
+        hi, lo = halves(jnp.where(fit256, out[64:96], 0.0))
+        row = pl.multiple_of((group // 2) * 128, 128) + (group % 2) * 32
+        mm_ref[pl.ds(pl.multiple_of(row, 32), 32), :] = hi
+        mm_ref[pl.ds(pl.multiple_of(row + 64, 32), 32), :] = lo
+        return 0
+
+    lax.fori_loop(0, GROUPS, image, 0, unroll=16)
 
     def natural(group, _):
         rows = pl.ds(pl.multiple_of(group * 64, 64), 64)
         hi, mid, lo = thirds(qs_ref[rows, :])
-        out = nn(jnp.concatenate([hi, mid, lo], axis=0), perm)
+        out = nn(jnp.concatenate([hi, mid, lo], axis=0), perm_ref[...])
         out = out[:64] + out[64:128] + out[128:]
         for i in range(4):
             for h in range(2):
@@ -348,12 +396,18 @@
         fill_face(d, wf, wsend)
         send_face(d, wline)
 
+    def split_w(group, _):
+        rows = pl.ds(pl.multiple_of(group * COLS, COLS), COLS)
+        by = [dsplit_ref[pl.ds(group * 2 + h, 1), :] for h in range(2)]
+        qs_ref[rows, :] = qs_ref[rows, :] * jnp.concatenate(by, axis=1)
+        return 0
+
+    lax.fori_loop(0, GROUPS, split_w, 0, unroll=4)
+
     def gram(left, right):
-        lh, ll = halves(left)
-        rh, rl = halves(right)
-        both = nt(jnp.concatenate([lh, ll], axis=0), rh)
-        n = left.shape[0]
-        return both[:n] + both[n:] + nt(lh, rl)
+        n, m = left.shape[0], right.shape[0]
+        out = nt(jnp.concatenate(halves(left), axis=0), jnp.concatenate(halves(right), axis=0))
+        return out[:n, :m] + (out[n:, :m] + (out[:n, m:] + out[n:, m:]))
 
     def product(step, sums):
         lanes = pl.ds(pl.multiple_of(step * 512, 512), 512)
@@ -363,11 +417,10 @@
         return sums[0] + n0, sums[1] + cw[:16], sums[2] + cw[16:]
 
     zero16 = jnp.zeros((COLS, COLS), F32)
-    grams = lax.fori_loop(0, 8, product, (zero16, zero16, zero16), unroll=4)
+    grams = lax.fori_loop(0, 8, product, (zero16, zero16, zero16), unroll=8)
 
     row16, lane16 = iota((COLS, LANES), 0), iota((COLS, LANES), 1)
     fits16 = row16 % 8 == lane16 // 16
-    sub8 = iota((8, LANES), 0)
     fits8 = sub8 == lane8 // 16
 
     def repeated(x):
@@ -421,96 +474,96 @@
     g1_ref[...] = packed
     red_send(0, g1_ref, g1_slots, along, nx)
 
-    def differ(r, _):
-        got = jnp.zeros((8, LANES), F32)
-        for k in range(1, 7):
-            there = jnp.broadcast_to(dext_ref[pl.ds(col_ref[k, r], 1), :], (8, LANES))
-            here = jnp.broadcast_to(dext_ref[pl.ds(r, 1), :], (8, LANES))
-            got = jnp.where(sub8 == k, here - there, got)
-        dd_ref[pl.ds(pl.multiple_of(r * 8, 8), 8), :] = got
-        return 0
-
-    lax.fori_loop(0, NODES, differ, 0, unroll=8)
-
-    k32, lane32 = iota((32, LANES), 0) % 8, iota((32, LANES), 1)
-    fit256 = iota((32, 256), 0) // 8 == iota((32, 256), 1) // DOF
-
-    def moved(group, _):
-        rows = pl.ds(pl.multiple_of(group * 32, 32), 32)
-        d = dd_ref[rows, :]
-        parts = []
-        for first, second in PAIRS:
-            keep = (k32 == first) & (lane32 < DOF)
-            if second is not None:
-                keep = keep | ((k32 == second) & (lane32 >= DOF))
-            parts.append(jnp.where(keep, d, 0.0))
-        hi, lo = halves(jnp.concatenate(parts, axis=1))
-        out = jnp.where(fit256, multiply(group, hi, lo, 4), 0.0)
-        hi, lo = halves(out)
-        out = nn(jnp.concatenate([hi, lo], axis=0), perm)
-        mvh_ref[rows, :] = out[:32].astype(BF16)
-        mvl_ref[rows, :] = out[32:].astype(BF16)
-        return 0
-
-    lax.fori_loop(0, GROUPS, moved, 0, unroll=4)
+    half = jnp.where(lo16, 0.5, 1.0)
+    block256 = iota((COLS, 256), 1) // DOF
+
+    def push(group, _):
+        w = qs_ref[pl.ds(pl.multiple_of(group * COLS, COLS), COLS), :]
+        left = jnp.concatenate([jnp.where(block256 == i, w, 0.0) for i in range(4)], axis=0)
+        base = pl.multiple_of(group * 512, 512)
+        left = jnp.concatenate(halves(left), axis=0)
+        a = nn(left, w_ref[pl.ds(base, 256), :256])
+        b = nn(left, w_ref[pl.ds(pl.multiple_of(base + 256, 256), 256), :256])
+        out = a[:64] + (a[64:] + (b[:64] + b[64:]))
+        for i in range(4):
+            rows = out[i * COLS : (i + 1) * COLS]
+            pushed_ref[group * 4 + i, :, :LANES] = rows[:, :LANES] * half
+            pushed_ref[group * 4 + i, :, LANES:] = rows[:, LANES:]
+        return 0
+
+    lax.fori_loop(0, GROUPS, push, 0, unroll=8)
 
     g2_ref[...] = red_sum(0, g1_ref, g1_slots, along)
     red_send(1, g2_ref, g2_slots, across, nb)
 
+    def within(step, total_):
+        left, high, low = [], [], []
+        for i in range(4):
+            r = step * 4 + i
+            left.append(pushed_ref[r])
+            for first, second in PAIRS[:2]:
+                a, b = col_ref[first, r], col_ref[second, r]
+                high.append(jnp.where(lo16, wh0[a], wh0[b]))
+                low.append(jnp.where(lo16, wl0[a], wl0[b]))
+        left = jnp.concatenate(halves(jnp.concatenate(left, axis=1)), axis=0)
+        right = jnp.concatenate([jnp.concatenate(high, axis=1), jnp.concatenate(low, axis=1)], axis=0)
+        out = nt(left, right)
+        return total_ + out[:16, :16] + (out[16:, :16] + (out[:16, 16:] + out[16:, 16:]))
+
+    inside = lax.fori_loop(0, GROUPS, within, zero16, unroll=16)
+    unit = jnp.where(iota((COLS, COLS), 0) == iota((COLS, COLS), 1), 1.0, 0.0)
+    inside = inside + exact_nt(unit, inside)
+
+    for at, (d, tile, upper) in enumerate(((1, 0, True), (3, 1, False), (5, 1, True))):
+        for q in range(8):
+            a = pushed_ref[face_ref[d, 2 * q], :, tile * LANES : (tile + 1) * LANES]
+            b = pushed_ref[face_ref[d, 2 * q + 1], :, tile * LANES : (tile + 1) * LANES]
+            x = jnp.where(lo16, pltpu.roll(a, DOF, 1), b) if upper else jnp.where(lo16, a, pltpu.roll(b, DOF, 1))
+            out_ref[:, (at * 8 + q) * LANES : (at * 8 + q + 1) * LANES] = x
+
     for d in (1, 3, 5):
         await_face(d, wline)
-    for d in (1, 3, 5):
-        take_face(d, wline, wf, wh0, wl0)
-
-    half = jnp.where(lo16, 0.5, 1.0).astype(BF16)
-
-    def curve(group, total_):
-        out = multiply(group, gathered(group, wh0, 2, half), gathered(group, wl0, 2, half), 2)
-        y = own_part(out)
-        w = qs_ref[pl.ds(pl.multiple_of(group * COLS, COLS), COLS), :]
-        w = w * jnp.concatenate(
-            [dsplit_ref[pl.ds(group * 2, 1), :], dsplit_ref[pl.ds(group * 2 + 1, 1), :]], axis=1
-        )
-        yh, yl = halves(y)
-        wh_, wl_ = halves(w)
-        a = nt(jnp.concatenate([wh_, wl_], axis=0), yh)
-        b = nt(jnp.concatenate([yh, yl], axis=0), wh_)
-        return total_ + a[:16] + a[16:] + b[:16] + b[16:] + nt(wh_, yl) + nt(yh, wl_)
-
-    curved = lax.fori_loop(0, GROUPS, curve, zero16, unroll=4)
+    curved = inside
+    for at, d in enumerate((1, 3, 5)):
+        there = jnp.concatenate([wrecv[d, q * COLS : (q + 1) * COLS, :] for q in range(8)], axis=1)
+        here = out_ref[:, at * 1024 : (at + 1) * 1024]
+        curved = curved + (gram(here, there) + gram(there, here))
     x1_ref[...] = jnp.concatenate(flattened(curved), axis=0)
     red_send(2, x1_ref, x1_slots, along, nx)
 
-    kinds = [(iota((COLS, LANES), 1) // 32, iota((COLS, LANES), 1) % 8)]
+    def moved_natural(four, _):
+        rows = pl.ds(pl.multiple_of(four * 256, 256), 256)
+        mv_ref[rows, :] = nn(mm_ref[rows, :], perm_ref[...]).astype(BF16)
+        return 0
+
+    lax.fori_loop(0, 4, moved_natural, 0, unroll=4)
+
+    pair_at, kind = iota((COLS, LANES), 1) // 32 % 2, iota((COLS, LANES), 1) % 8
 
     def terms(four, base, full):
-        rows = pl.ds(pl.multiple_of(four * LANES, LANES), LANES)
-        mh, ml = mvh_ref[rows, :], mvl_ref[rows, :]
-        got = jnp.zeros((COLS, LANES), F32)
-        for g in range(4):
-            r = (four * 4 + g) * 4
-            here = [jnp.where(lo16, full[r + 2 * h], full[r + 2 * h + 1]) for h in range(2)]
-            parts = []
-            for k in range(1, 7):
-                parts.append(
-                    jnp.concatenate(
-                        [
-                            here[h]
-                            - jnp.where(
-                                lo16, full[col_ref[k, r + 2 * h]], full[col_ref[k, r + 2 * h + 1]]
-                            )
-                            for h in range(2)
-                        ],
-                        axis=1,
-                    )
-                )
-            hi, lo = halves(jnp.concatenate(parts, axis=0))
-            both = nt(jnp.concatenate([hi, lo], axis=0), mh)
-            out = both[:96] + both[96:] + nt(hi, ml)
-            for k in range(1, 7):
-                keep = (kinds[0][0] == g) & (kinds[0][1] == k)
-                got = got + jnp.where(keep, out[(k - 1) * COLS : k * COLS], 0.0)
-        term_ref[base : base + COLS, pl.ds(pl.multiple_of(four * LANES, LANES), LANES)] = 0.5 * got
+        pairs = []
+        for pair in range(2):
+            weights = mv_ref[pl.ds(pl.multiple_of(four * 256, 256) + pair * 128, 128), :]
+            got = jnp.zeros((COLS, LANES), F32)
+            for g in range(2):
+                r = (four * 4 + pair * 2 + g) * 4
+                here = [jnp.where(lo16, full[r + 2 * h], full[r + 2 * h + 1]) for h in range(2)]
+                parts = []
+                for k in range(1, 7):
+                    there = [
+                        jnp.where(lo16, full[col_ref[k, r + 2 * h]], full[col_ref[k, r + 2 * h + 1]])
+                        for h in range(2)
+                    ]
+                    parts.append(jnp.concatenate([here[h] - there[h] for h in range(2)], axis=1))
+                hi, lo = halves(jnp.concatenate(parts, axis=0))
+                out = nt(jnp.concatenate([hi, lo], axis=0), weights)
+                out = out[:96] + out[96:]
+                for k in range(1, 7):
+                    keep = (pair_at == g) & (kind == k)
+                    got = jnp.where(keep, out[(k - 1) * COLS : k * COLS], got)
+            pairs.append(got + pltpu.roll(got, DOF, 1))
+        lanes = pl.ds(pl.multiple_of(four * LANES, LANES), LANES)
+        term_ref[base : base + COLS, lanes] = 0.5 * jnp.where(lo16, pairs[0], pairs[1])
 
     def terms_z(four, _):
         terms(four, 0, zf)
@@ -520,16 +573,73 @@
         terms(four, COLS, wf)
         return 0
 
-    lax.fori_loop(0, 4, terms_z, 0)
+    def solved(x, panel=4):
+        n = x.shape[0]
+        lane = iota((1, LANES), 1) % COLS
+        for first in range(0, COLS, panel):
+            cols = [
+                jnp.broadcast_to(x[:, k : k + 1], (n, LANES)) for k in range(first, first + panel)
+            ]
+            for j in range(panel):
+                k = first + j
+                scaled = cols[j] * (1.0 / cols[j][k : k + 1, :])
+                cols = [
+                    scaled if i == j else c - scaled * c[k : k + 1, :] for i, c in enumerate(cols)
+                ]
+            new = x
+            for j in range(panel):
+                new = new - cols[j] * x[first + j : first + j + 1, :]
+            for j in range(panel):
+                new = jnp.where(lane == first + j, cols[j], new)
+            x = new
+        return x[COLS:]
+
+    g = red_sum(1, g2_ref, g2_slots, across)
+    n0 = unflattened([g[0:1], g[1:2]])
+    c0 = unflattened([g[2:3], g[3:4]])
+    w0 = unflattened([g[4:5], g[5:6]])
+    first = solved(jnp.concatenate([c0, n0, w0], axis=0))
+    step0, mix = first[:COLS], first[COLS:]
+    low16 = lane16 < COLS
+    step0_, mix_ = jnp.where(low16, step0, 0.0), jnp.where(low16, mix, 0.0)
+
+    pad = jnp.zeros((LANES - COLS, LANES), F32)
+
+    def times(a, b):
+        return exact_nn(a, jnp.concatenate([b, pad], axis=0))
+
+    mix_w = times(mix_, w0)
+    right = times(step0_, w0) - c0
+
+    both = jnp.concatenate([step0[:, :COLS], mix[:, :COLS]], axis=0)
+    bh, bm, bl = thirds(both)
+    lhs = jnp.concatenate([bh, bh, bm, bh, bm, bl], axis=1)
+
+    def prepare(step, _):
+        lanes = pl.ds(pl.multiple_of(step * 512, 512), 512)
+        ah, am, al = thirds(zp_ref[:, lanes])
+        out = nn(lhs, jnp.concatenate([ah, am, ah, al, am, ah], axis=0))
+        xa_ref[:, lanes] = out[:16]
+        ah, am, al = thirds(out[16:] - wp_ref[:, lanes])
+        vp_ref[0:16, lanes] = ah
+        vp_ref[16:32, lanes] = am
+        vp_ref[32:48, lanes] = al
+        return 0
+
+    lax.fori_loop(0, 8, prepare, 0, unroll=8)
 
     x2_ref[...] = red_sum(2, x1_ref, x1_slots, along)
     red_send(3, x2_ref, x2_slots, across, nb)
 
+    lax.fori_loop(0, 4, terms_z, 0, unroll=4)
+
+
     for d in (0, 2, 4):
         await_face(d, wline)
-    for d in (0, 2, 4):
-        take_face(d, wline, wf, wh0, wl0)
-    lax.fori_loop(0, 4, terms_w, 0)
+    for d in range(6):
+        for q in range(8):
+            put_full(wrecv[d, q * COLS : (q + 1) * COLS, :], NODES + d * 16 + 2 * q, wf)
+    lax.fori_loop(0, 4, terms_w, 0, unroll=4)
 
     hi, mid, lo = thirds(term_ref[...])
     sums = nt(jnp.concatenate([hi, mid, lo], axis=0), oh_ref[...])
@@ -542,49 +652,6 @@
     )
     carry.start()
 
-    def solved(x):
-        n = x.shape[0]
-        lane = iota((1, LANES), 1) % COLS
-        for k in range(COLS):
-            inv = 1.0 / x[k : k + 1, k : k + 1]
-            column = jnp.broadcast_to(x[:, k : k + 1], (n, LANES)) * inv
-            x = jnp.where(lane == k, column, x - column * jnp.broadcast_to(x[k : k + 1, :], (n, LANES)))
-        return x[COLS:]
-
-    g = red_sum(1, g2_ref, g2_slots, across)
-    n0 = unflattened([g[0:1], g[1:2]])
-    c0 = unflattened([g[2:3], g[3:4]])
-    w0 = unflattened([g[4:5], g[5:6]])
-    first = solved(jnp.concatenate([c0, n0, w0], axis=0))
-    step0, mix = first[:COLS], first[COLS:]
-    low16 = lane16 < COLS
-    step0_, mix_ = jnp.where(low16, step0, 0.0), jnp.where(low16, mix, 0.0)
-
-    pad = jnp.zeros((LANES - COLS, LANES), F32)
-
-    def times(a, b):
-        return exact_nn(a, jnp.concatenate([b, pad], axis=0))
-
-    mix_w = times(mix_, w0)
-    right = times(step0_, w0) - c0
-
-    both = jnp.concatenate([step0[:, :COLS], mix[:, :COLS]], axis=0)
-    bh, bm, bl = thirds(both)
-    lhs = jnp.concatenate([bh, bh, bm, bh, bm, bl], axis=1)
-
-    def prepare(step, _):
-        lanes = pl.ds(pl.multiple_of(step * 512, 512), 512)
-        ah, am, al = thirds(zp_ref[:, lanes])
-        out = nn(lhs, jnp.concatenate([ah, am, ah, al, am, ah], axis=0))
-        xa_ref[:, lanes] = out[:16]
-        ah, am, al = thirds(out[16:] - wp_ref[:, lanes])
-        vp_ref[0:16, lanes] = ah
-        vp_ref[16:32, lanes] = am
-        vp_ref[32:48, lanes] = al
-        return 0
-
-    lax.fori_loop(0, 8, prepare, 0, unroll=2)
-
     carry.wait_recv()
     all_sums = own_sums + carry_ref[...]
     ah, am, al = thirds(all_sums[:16])
@@ -606,7 +673,7 @@
         adj_ref[:, lanes] = xa_ref[:, lanes] + out
         return 0
 
-    lax.fori_loop(0, 8, finish, 0, unroll=4)
+    lax.fori_loop(0, 8, finish, 0, unroll=8)
     ah, am, al = sens_v
     sens_ref[...] = sens_a + nn(lhs, jnp.concatenate([ah, am, ah, al, am, ah], axis=0))
 
@@ -626,7 +693,6 @@
     tiles = jnp.transpose(stiffness, (1, 0, 2)).reshape(7, 8, 8, 32, LANES)
     tiles = jnp.transpose(tiles, (0, 1, 3, 2, 4)).reshape(7 * 8 * 32 * 8, LANES)
     vmem = pl.BlockSpec(memory_space=pltpu.VMEM)
-    smem = pl.BlockSpec(memory_space=pltpu.SMEM)
     dma = pltpu.SemaphoreType.DMA
     v = pltpu.VMEM
     return pl.pallas_call(
@@ -635,11 +701,12 @@
             jax.ShapeDtypeStruct((COLS, NODES * DOF), F32),
             jax.ShapeDtypeStruct((COLS, ZONE_DEV), F32),
         ),
-        in_specs=[vmem, vmem, pl.BlockSpec(memory_space=pl.ANY), smem, smem, vmem],
+        in_specs=[pl.BlockSpec(memory_space=pl.ANY)] * 6,
         out_specs=(vmem, vmem),
         scratch_shapes=[
-            v((7 * 8 * 32 * 8, LANES), F32),
-            v((NODES * DOF, 512), BF16), v((NODES * DOF, 512), BF16),
+            v((COLS, NODES * DOF), F32), v((32, LANES), F32), pltpu.SMEM((7, NODES), jnp.int32),
+            pltpu.SMEM((6, 16), jnp.int32), v((6, NODES), jnp.int32),
+            v((7 * 8 * 32 * 8, LANES), F32), v((2 * NODES * DOF, 512), BF16),
             v((EXT, COLS, LANES), F32), v((EXT, COLS, LANES), BF16), v((EXT, COLS, LANES), BF16),
             v((EXT, COLS, LANES), F32), v((EXT, COLS, LANES), BF16), v((EXT, COLS, LANES), BF16),
             v((COLS, NODES * DOF), F32), v((GROUPS * COLS, 256), F32),
@@ -647,8 +714,8 @@
             v((3 * COLS, NODES * DOF), BF16), v((COLS, NODES * DOF), F32),
             v((NODES, LANES), F32), v((32, LANES), F32), v((32, LANES), F32),
             v((EXT, LANES), F32), v((NODES * 8, LANES), F32),
-            v((NODES * 8, 256), BF16), v((NODES * 8, 256), BF16),
-            v((2 * ZONE_DEV, 512), BF16), v((2 * COLS, 512), F32),
+            v((2 * NODES * 8, 256), BF16), v((2 * NODES * 8, 256), BF16), v((NODES, COLS, 256), F32),
+            v((COLS, 3 * 1024), F32), v((2 * ZONE_DEV, 512), BF16), v((2 * COLS, 512), F32), v((256, 256), BF16),
             v((6, FACE_ROWS, LANES), F32), v((6, 8 * COLS, LANES), F32),
             v((6, FACE_ROWS, LANES), F32), v((6, 8 * COLS, LANES), F32),
             v((8, LANES), F32), v((8, LANES), F32),
@@ -656,11 +723,11 @@
             v((2, LANES), F32), v((2, LANES), F32),
             v((nx - 1, 2, LANES), F32), v((nb - 1, 2, LANES), F32),
             v((2 * COLS, ZONE_DEV), F32), v((2 * COLS, ZONE_DEV), F32),
-            dma((7,)), dma((6,)), dma((6,)), dma((6,)), dma((6,)),
+            dma((7,)), dma((5,)), dma((6,)), dma((6,)), dma((6,)), dma((6,)),
             dma((4,)), dma((4,)), dma((2,)),
         ],
         compiler_params=pltpu.CompilerParams(
-            collective_id=0, has_side_effects=True, vmem_limit_bytes=48 * 1024 * 1024
+            collective_id=0, has_side_effects=True, vmem_limit_bytes=63 * 1024 * 1024
         ),
         cost_estimate=pl.CostEstimate(
             flops=400_000_000, bytes_accessed=8_000_000, transcendentals=0

time: 53.5 us -> 44 us (0.82)
  Pallas kernels: 47.5 us -> 40.3 us
  local copies, waits for them, and re-layouts: 5.02 us -> 2.97 us
    pallas_call x1, Pallas kernels: 47.5 us -> 40.3 us  [on_device(): pl.pallas_call(functools.partial(kernel, sizes), out_shape=(jax.ShapeDtyp...]
    unnamed x12 -> x2, local copies, waits for them, and re-layouts: 5.02 us -> 2.97 us
where the time goes in v2:
time: 44 us; the launch traced here: 43.9 us
  Pallas kernels  40.3 us (92%)
  local copies, waits for them, and re-layouts  2.97 us (7%)
  between operations  0.64 us (1%)
    pallas_call x1, Pallas kernels, on_device(): pl.pallas_call(functools.partial(kernel, sizes), out_shape=(jax.ShapeDtyp...  40.3 us
    unnamed x2, local copies, waits for them, and re-layouts  2.97 us

profile of v2, /device:TPU:1, one launch (start us, length us, event | category | flops | bytes accessed | tf_op | source)
XLA Modules:
  0.0 43.9 jit_solution(8179684966184131826)
XLA Ops:
  0.6 40.3 %shard_map.77 = (f32[16,4096]{1,0:T(8,128)}, f32[16,128]{1,0:T(8,128)}) custom-call(f32[16,4096]{1,0:T(8,128)} %loads_in.1, f32[32,128]{1,0:T(8,128)} %bitcast.11, f32[14336,128]{1,0:T(8,128)} %bitcast.10, s32[7,64]{1,0:T(8,128)} %bitcast.12, s32[6,16]{1,0:T(8,128)} %face_in.1, s32[6,64]{1,0:T(8,128)} %bitcast.13), custom_call_target="tpu_custom_call" | custom-call | flops 400000000 | bytes 8000000 | tf_op jit(solution)/shard_map/pallas_call | solution.py:698
  40.9 1.7 %copy.10 = f32[16,4096]{1,0:T(8,128)} copy(f32[16,4096]{1,0:T(8,128)} %get-tuple-element.4) | data formatting | bytes 524288
  42.6 1.3 %copy.11 = f32[16,128]{1,0:T(8,128)} copy(f32[16,128]{1,0:T(8,128)} %get-tuple-element.5) | data formatting | bytes 16384

commit v3 on v2

--- a/solution.py
+++ b/solution.py
@@ -68,11 +68,11 @@
     loads_ref, disp_ref, col_ref, face_ref, zone_ref,
     m_ref, w_ref,
     zf, zh, zl, wf, wh0, wl0,
-    zp_ref, qs_ref, qp_ref, wp_ref, vp_ref, xa_ref,
+    zp_ref, qs_ref, qp_ref, wp_ref, vp_ref,
     dinv_ref, dpack_ref, dsplit_ref, dext_ref, dd_ref,
     mm_ref, mv_ref, pushed_ref, out_ref, oh_ref, term_ref, perm_ref,
     zsend, wsend, zrecv, wrecv,
-    g1_ref, g2_ref, g1_slots, g2_slots, x1_ref, x2_ref, x1_slots, x2_slots,
+    g1_ref, g2_ref, g1_slots, g2_slots,
     part_ref, carry_ref,
     load_sems, input_sems, z_send_sems, z_recv_sems, w_send_sems, w_recv_sems,
     red_send_sems, red_recv_sems, carry_sems,
@@ -95,13 +95,6 @@
         s = lax.rem(me + i + total, total)
         b = lax.rem(s, nb)
         return (s // nb, b // nz, lax.rem(b, nz))
-
-    barrier = pltpu.get_barrier_semaphore()
-    for i in range(1, nx):
-        pl.semaphore_signal(barrier, inc=1, device_id=along(i), device_id_type=MESH)
-    for i in range(1, nb):
-        pl.semaphore_signal(barrier, inc=1, device_id=across(i), device_id_type=MESH)
-    pl.semaphore_signal(barrier, inc=1, device_id=flat(-1), device_id_type=MESH)
 
     rows_k = NODES // 8 * 32 * 8
 
@@ -123,6 +116,13 @@
         for k in pair:
             if k:
                 stiff_copy(k).start()
+
+    barrier = pltpu.get_barrier_semaphore()
+    for i in range(1, nx):
+        pl.semaphore_signal(barrier, inc=1, device_id=along(i), device_id_type=MESH)
+    for i in range(1, nb):
+        pl.semaphore_signal(barrier, inc=1, device_id=across(i), device_id_type=MESH)
+    pl.semaphore_signal(barrier, inc=1, device_id=flat(-1), device_id_type=MESH)
 
     lo16, lo8, lo32 = lower(), lower(8), lower(32)
 
@@ -337,39 +337,12 @@
         )
 
     sub8 = iota((8, LANES), 0)
-    def differ(r, _):
-        got = jnp.zeros((8, LANES), F32)
-        for k in range(1, 7):
-            there = jnp.broadcast_to(dext_ref[pl.ds(col_ref[k, r], 1), :], (8, LANES))
-            here = jnp.broadcast_to(dext_ref[pl.ds(r, 1), :], (8, LANES))
-            got = jnp.where(sub8 == k, here - there, got)
-        dd_ref[pl.ds(pl.multiple_of(r * 8, 8), 8), :] = got
-        return 0
-
-    lax.fori_loop(0, NODES, differ, 0, unroll=16)
-
-    k32, lane32 = iota((32, LANES), 0) % 8, iota((32, LANES), 1)
-    fit256 = iota((32, 256), 0) // 8 == iota((32, 256), 1) // DOF
-
     def image(group, _):
-        small = pl.ds(pl.multiple_of(group * 32, 32), 32)
-        d = dd_ref[small, :]
-        parts = []
-        for first, second in PAIRS:
-            keep = (k32 == first) & (lane32 < DOF)
-            if second is not None:
-                keep = keep | ((k32 == second) & (lane32 >= DOF))
-            parts.append(jnp.where(keep, d, 0.0))
-        hi, lo = halves(jnp.concatenate(parts, axis=1))
         rows = pl.ds(pl.multiple_of(group * 512, 512), 512)
-        left = jnp.concatenate([gathered(group, zh), hi, gathered(group, zl), lo], axis=0)
+        left = jnp.concatenate([gathered(group, zh), gathered(group, zl)], axis=0)
         out = nt(left, w_ref[rows, :])
-        out = out[:96, :256] + (out[96:, :256] + (out[:96, 256:] + out[96:, 256:]))
+        out = out[:64, :256] + (out[64:, :256] + (out[:64, 256:] + out[64:, 256:]))
         qs_ref[pl.ds(pl.multiple_of(group * COLS, COLS), COLS), :] = own_part(out)
-        hi, lo = halves(jnp.where(fit256, out[64:96], 0.0))
-        row = pl.multiple_of((group // 2) * 128, 128) + (group % 2) * 32
-        mm_ref[pl.ds(pl.multiple_of(row, 32), 32), :] = hi
-        mm_ref[pl.ds(pl.multiple_of(row + 64, 32), 32), :] = lo
         return 0
 
     lax.fori_loop(0, GROUPS, image, 0, unroll=16)
@@ -467,13 +440,6 @@
             got = [a + b for a, b in zip(got[::2], got[1::2])] + got[len(got) & ~1 :]
         return got[0]
 
-    rows = flattened(grams[0]) + flattened(grams[1]) + flattened(grams[2])
-    packed = jnp.zeros((8, LANES), F32)
-    for i, row in enumerate(rows):
-        packed = jnp.where(sub8 == i, jnp.broadcast_to(row, (8, LANES)), packed)
-    g1_ref[...] = packed
-    red_send(0, g1_ref, g1_slots, along, nx)
-
     half = jnp.where(lo16, 0.5, 1.0)
     block256 = iota((COLS, 256), 1) // DOF
 
@@ -492,9 +458,6 @@
         return 0
 
     lax.fori_loop(0, GROUPS, push, 0, unroll=8)
-
-    g2_ref[...] = red_sum(0, g1_ref, g1_slots, along)
-    red_send(1, g2_ref, g2_slots, across, nb)
 
     def within(step, total_):
         left, high, low = [], [], []
@@ -514,6 +477,11 @@
     unit = jnp.where(iota((COLS, COLS), 0) == iota((COLS, COLS), 1), 1.0, 0.0)
     inside = inside + exact_nt(unit, inside)
 
+    rows = flattened(grams[0]) + flattened(grams[1]) + flattened(grams[2])
+    packed_early = jnp.zeros((8, LANES), F32)
+    for i, row in enumerate(rows):
+        packed_early = jnp.where(sub8 == i, jnp.broadcast_to(row, (8, LANES)), packed_early)
+
     for at, (d, tile, upper) in enumerate(((1, 0, True), (3, 1, False), (5, 1, True))):
         for q in range(8):
             a = pushed_ref[face_ref[d, 2 * q], :, tile * LANES : (tile + 1) * LANES]
@@ -528,8 +496,45 @@
         there = jnp.concatenate([wrecv[d, q * COLS : (q + 1) * COLS, :] for q in range(8)], axis=1)
         here = out_ref[:, at * 1024 : (at + 1) * 1024]
         curved = curved + (gram(here, there) + gram(there, here))
-    x1_ref[...] = jnp.concatenate(flattened(curved), axis=0)
-    red_send(2, x1_ref, x1_slots, along, nx)
+    packed = packed_early
+    for i, row in enumerate(flattened(curved)):
+        packed = jnp.where(sub8 == 6 + i, jnp.broadcast_to(row, (8, LANES)), packed)
+    g1_ref[...] = packed
+    red_send(0, g1_ref, g1_slots, along, nx)
+
+    def differ(r, _):
+        got = jnp.zeros((8, LANES), F32)
+        for k in range(1, 7):
+            there = jnp.broadcast_to(dext_ref[pl.ds(col_ref[k, r], 1), :], (8, LANES))
+            here = jnp.broadcast_to(dext_ref[pl.ds(r, 1), :], (8, LANES))
+            got = jnp.where(sub8 == k, here - there, got)
+        dd_ref[pl.ds(pl.multiple_of(r * 8, 8), 8), :] = got
+        return 0
+
+    lax.fori_loop(0, NODES, differ, 0, unroll=16)
+
+    k32, lane32 = iota((32, LANES), 0) % 8, iota((32, LANES), 1)
+    fit256 = iota((32, 256), 0) // 8 == iota((32, 256), 1) // DOF
+
+    def moved(group, _):
+        small = pl.ds(pl.multiple_of(group * 32, 32), 32)
+        d = dd_ref[small, :]
+        parts = []
+        for first, second in PAIRS:
+            keep = (k32 == first) & (lane32 < DOF)
+            if second is not None:
+                keep = keep | ((k32 == second) & (lane32 >= DOF))
+            parts.append(jnp.where(keep, d, 0.0))
+        left = jnp.concatenate(halves(jnp.concatenate(parts, axis=1)), axis=0)
+        out = nt(left, w_ref[pl.ds(pl.multiple_of(group * 512, 512), 512), :])
+        out = out[:32, :256] + (out[32:, :256] + (out[:32, 256:] + out[32:, 256:]))
+        hi, lo = halves(jnp.where(fit256, out, 0.0))
+        row = pl.multiple_of((group // 2) * 128, 128) + (group % 2) * 32
+        mm_ref[pl.ds(pl.multiple_of(row, 32), 32), :] = hi
+        mm_ref[pl.ds(pl.multiple_of(row + 64, 32), 32), :] = lo
+        return 0
+
+    lax.fori_loop(0, GROUPS, moved, 0, unroll=16)
 
     def moved_natural(four, _):
         rows = pl.ds(pl.multiple_of(four * 256, 256), 256)
@@ -537,6 +542,10 @@
         return 0
 
     lax.fori_loop(0, 4, moved_natural, 0, unroll=4)
+
+    g2_ref[...] = red_sum(0, g1_ref, g1_slots, along)
+    red_send(1, g2_ref, g2_slots, across, nb)
+
 
     pair_at, kind = iota((COLS, LANES), 1) // 32 % 2, iota((COLS, LANES), 1) % 8
 
@@ -573,7 +582,43 @@
         terms(four, COLS, wf)
         return 0
 
-    def solved(x, panel=4):
+
+    lax.fori_loop(0, 4, terms_z, 0, unroll=4)
+
+    for d in (0, 2, 4):
+        await_face(d, wline)
+    for d in range(6):
+        for q in range(8):
+            put_full(wrecv[d, q * COLS : (q + 1) * COLS, :], NODES + d * 16 + 2 * q, wf)
+    lax.fori_loop(0, 4, terms_w, 0, unroll=4)
+
+    hi, mid, lo = thirds(term_ref[...])
+    sums = nt(jnp.concatenate([hi, mid, lo], axis=0), oh_ref[...])
+    sums = sums[:32] + sums[32:64] + sums[64:]
+    own_sums = sums[:, :ZONE_DEV]
+    part_ref[...] = sums[:, ZONE_DEV:]
+    carry = pltpu.make_async_remote_copy(
+        src_ref=part_ref, dst_ref=carry_ref, send_sem=carry_sems.at[0], recv_sem=carry_sems.at[1],
+        device_id=flat(1), device_id_type=MESH,
+    )
+    carry.start()
+
+    def stacked(z, w):
+        ah, am, al = thirds(jnp.concatenate([z, w], axis=0))
+        return jnp.concatenate([ah, am, ah, al, am, ah], axis=0)
+
+    def prepare(step, _):
+        lanes = pl.ds(pl.multiple_of(step * 512, 512), 512)
+        vp_ref[:, lanes] = stacked(zp_ref[:, lanes], wp_ref[:, lanes])
+        return 0
+
+    lax.fori_loop(0, 8, prepare, 0, unroll=8)
+
+    carry.wait_recv()
+    all_sums = own_sums + carry_ref[...]
+    sens_right = stacked(all_sums[:COLS], all_sums[COLS:])
+
+    def solved(x, panel=16):
         n = x.shape[0]
         lane = iota((1, LANES), 1) % COLS
         for first in range(0, COLS, panel):
@@ -611,80 +656,44 @@
     mix_w = times(mix_, w0)
     right = times(step0_, w0) - c0
 
-    both = jnp.concatenate([step0[:, :COLS], mix[:, :COLS]], axis=0)
-    bh, bm, bl = thirds(both)
-    lhs = jnp.concatenate([bh, bh, bm, bh, bm, bl], axis=1)
-
-    def prepare(step, _):
-        lanes = pl.ds(pl.multiple_of(step * 512, 512), 512)
-        ah, am, al = thirds(zp_ref[:, lanes])
-        out = nn(lhs, jnp.concatenate([ah, am, ah, al, am, ah], axis=0))
-        xa_ref[:, lanes] = out[:16]
-        ah, am, al = thirds(out[16:] - wp_ref[:, lanes])
-        vp_ref[0:16, lanes] = ah
-        vp_ref[16:32, lanes] = am
-        vp_ref[32:48, lanes] = al
-        return 0
-
-    lax.fori_loop(0, 8, prepare, 0, unroll=8)
-
-    x2_ref[...] = red_sum(2, x1_ref, x1_slots, along)
-    red_send(3, x2_ref, x2_slots, across, nb)
-
-    lax.fori_loop(0, 4, terms_z, 0, unroll=4)
-
-
-    for d in (0, 2, 4):
-        await_face(d, wline)
-    for d in range(6):
-        for q in range(8):
-            put_full(wrecv[d, q * COLS : (q + 1) * COLS, :], NODES + d * 16 + 2 * q, wf)
-    lax.fori_loop(0, 4, terms_w, 0, unroll=4)
-
-    hi, mid, lo = thirds(term_ref[...])
-    sums = nt(jnp.concatenate([hi, mid, lo], axis=0), oh_ref[...])
-    sums = sums[:32] + sums[32:64] + sums[64:]
-    own_sums = sums[:, :ZONE_DEV]
-    part_ref[...] = sums[:, ZONE_DEV:]
-    carry = pltpu.make_async_remote_copy(
-        src_ref=part_ref, dst_ref=carry_ref, send_sem=carry_sems.at[0], recv_sem=carry_sems.at[1],
-        device_id=flat(1), device_id_type=MESH,
-    )
-    carry.start()
-
-    carry.wait_recv()
-    all_sums = own_sums + carry_ref[...]
-    ah, am, al = thirds(all_sums[:16])
-    out = nn(lhs, jnp.concatenate([ah, am, ah, al, am, ah], axis=0))
-    sens_a = out[:16]
-    sens_v = thirds(out[16:] - all_sums[16:])
-
-    x = red_sum(3, x2_ref, x2_slots, across)
-    x = unflattened([x[0:1], x[1:2]])
-    y = solved(jnp.concatenate([x - mix_w, right], axis=0))[:, :COLS]
-    yh, ym, yl = thirds(y)
+    x = unflattened([g[6:7], g[7:8]])
+    y = solved(jnp.concatenate([x - mix_w, right], axis=0))
+    y_ = jnp.where(low16, y, 0.0)
+    both = jnp.concatenate([(step0 + times(y_, mix))[:, :COLS], -y[:, :COLS]], axis=1)
+    yh, ym, yl = thirds(both)
     lhs = jnp.concatenate([yh, yh, ym, yh, ym, yl], axis=1)
 
     def finish(step, _):
         lanes = pl.ds(pl.multiple_of(step * 512, 512), 512)
-        v = vp_ref[:, lanes]
-        ah, am, al = v[0:16], v[16:32], v[32:48]
-        out = nn(lhs, jnp.concatenate([ah, am, ah, al, am, ah], axis=0))
-        adj_ref[:, lanes] = xa_ref[:, lanes] + out
+        adj_ref[:, lanes] = nn(lhs, vp_ref[:, lanes])
         return 0
 
     lax.fori_loop(0, 8, finish, 0, unroll=8)
-    ah, am, al = sens_v
-    sens_ref[...] = sens_a + nn(lhs, jnp.concatenate([ah, am, ah, al, am, ah], axis=0))
+    sens_ref[...] = nn(lhs, sens_right)
 
     for d in range(6):
         end_face(d, zline)
         end_face(d, wline)
     red_all(0, g1_slots, along).wait_send()
     red_all(1, g2_slots, across).wait_send()
-    red_all(2, x1_slots, along).wait_send()
-    red_all(3, x2_slots, across).wait_send()
     carry.wait_send()
+
+
+def settle(adj_in, sens_in, adj_out, sens_out, adj_ref, sens_ref, sems):
+    pieces = [(sens_in, sens_ref, sens_out)]
+    for i in range(2):
+        for j in range(4):
+            part = (pl.ds(i * 8, 8), pl.ds(j * 1024, 1024))
+            pieces.append((adj_in.at[part], adj_ref.at[part], adj_out.at[part]))
+    come = [pltpu.make_async_copy(a, b, sems.at[0, i]) for i, (a, b, _) in enumerate(pieces)]
+    go = [pltpu.make_async_copy(b, c, sems.at[1, i]) for i, (_, b, c) in enumerate(pieces)]
+    for copy in come:
+        copy.start()
+    for one, other in zip(come, go):
+        one.wait()
+        other.start()
+    for copy in go:
+        copy.wait()
 
 
 def on_device(sizes, loads, displacement, stiffness, col_index, face_index, zone_map):
@@ -695,7 +704,7 @@
     vmem = pl.BlockSpec(memory_space=pltpu.VMEM)
     dma = pltpu.SemaphoreType.DMA
     v = pltpu.VMEM
-    return pl.pallas_call(
+    results = pl.pallas_call(
         functools.partial(kernel, sizes),
         out_shape=(
             jax.ShapeDtypeStruct((COLS, NODES * DOF), F32),
@@ -711,7 +720,7 @@
             v((EXT, COLS, LANES), F32), v((EXT, COLS, LANES), BF16), v((EXT, COLS, LANES), BF16),
             v((COLS, NODES * DOF), F32), v((GROUPS * COLS, 256), F32),
             v((COLS, NODES * DOF), F32), v((COLS, NODES * DOF), F32),
-            v((3 * COLS, NODES * DOF), BF16), v((COLS, NODES * DOF), F32),
+            v((12 * COLS, NODES * DOF), BF16),
             v((NODES, LANES), F32), v((32, LANES), F32), v((32, LANES), F32),
             v((EXT, LANES), F32), v((NODES * 8, LANES), F32),
             v((2 * NODES * 8, 256), BF16), v((2 * NODES * 8, 256), BF16), v((NODES, COLS, 256), F32),
@@ -720,11 +729,9 @@
             v((6, FACE_ROWS, LANES), F32), v((6, 8 * COLS, LANES), F32),
             v((8, LANES), F32), v((8, LANES), F32),
             v((nx - 1, 8, LANES), F32), v((nb - 1, 8, LANES), F32),
-            v((2, LANES), F32), v((2, LANES), F32),
-            v((nx - 1, 2, LANES), F32), v((nb - 1, 2, LANES), F32),
             v((2 * COLS, ZONE_DEV), F32), v((2 * COLS, ZONE_DEV), F32),
             dma((7,)), dma((5,)), dma((6,)), dma((6,)), dma((6,)), dma((6,)),
-            dma((4,)), dma((4,)), dma((2,)),
+            dma((2,)), dma((2,)), dma((2,)),
         ],
         compiler_params=pltpu.CompilerParams(
             collective_id=0, has_side_effects=True, vmem_limit_bytes=63 * 1024 * 1024
@@ -736,6 +743,18 @@
         loads, displacement.reshape(32, LANES), tiles,
         jnp.transpose(col_index), face_index, jnp.transpose(zone_map),
     )
+    hbm = pl.BlockSpec(memory_space=pl.ANY)
+    return pl.pallas_call(
+        settle,
+        out_shape=(
+            jax.ShapeDtypeStruct((COLS, NODES * DOF), F32),
+            jax.ShapeDtypeStruct((COLS, ZONE_DEV), F32),
+        ),
+        in_specs=[hbm, hbm],
+        out_specs=(hbm, hbm),
+        scratch_shapes=[v((COLS, NODES * DOF), F32), v((COLS, ZONE_DEV), F32), dma((2, 9))],
+        compiler_params=pltpu.CompilerParams(vmem_limit_bytes=63 * 1024 * 1024),
+    )(*results)
 
 
 def solution(mesh):

time: 44 us -> 40.5 us (0.920)
  local copies, waits for them, and re-layouts: 2.97 us -> 0 us
  Pallas kernels: 40.3 us -> 39.7 us
    unnamed x2 -> x0, local copies, waits for them, and re-layouts: 2.97 us -> none
    pallas_call x1, Pallas kernels: 40.3 us -> 38.1 us  [on_device(): pl.pallas_call(functools.partial(kernel, sizes), out_shape=(jax.ShapeDtyp...]
    pallas_call x0 -> x1, Pallas kernels: none -> 1.66 us  [on_device(): pl.pallas_call(settle, out_shape=(jax.ShapeDtypeStruct((COLS, NODES * DOF...]
where the time goes in v3:
time: 40.5 us; the launch traced here: 40.4 us
  Pallas kernels  39.7 us (98%)
  between operations  0.64 us (2%)
    pallas_call x1, Pallas kernels, on_device(): pl.pallas_call(functools.partial(kernel, sizes), out_shape=(jax.ShapeDtyp...  38.1 us
    pallas_call x1, Pallas kernels, on_device(): pl.pallas_call(settle, out_shape=(jax.ShapeDtypeStruct((COLS, NODES * DOF...  1.66 us

profile of v3, /device:TPU:1, one launch (start us, length us, event | category | flops | bytes accessed | tf_op | source)
XLA Modules:
  0.0 40.4 jit_solution(1644894087106080563)
XLA Ops:
  0.6 38.1 %shard_map.77 = (f32[16,4096]{1,0:T(8,128)}, f32[16,128]{1,0:T(8,128)}) custom-call(f32[16,4096]{1,0:T(8,128)} %loads_in.1, f32[32,128]{1,0:T(8,128)} %bitcast.11, f32[14336,128]{1,0:T(8,128)} %bitcast.10, s32[7,64]{1,0:T(8,128)} %bitcast.12, s32[6,16]{1,0:T(8,128)} %face_in.1, s32[6,64]{1,0:T(8,128)} %bitcast.13), custom_call_target="tpu_custom_call" | custom-call | flops 400000000 | bytes 8000000 | tf_op jit(solution)/shard_map/pallas_call | solution.py:707
  38.7 1.7 %shard_map.78 = (f32[16,4096]{1,0:T(8,128)}, f32[16,128]{1,0:T(8,128)}) custom-call(f32[16,4096]{1,0:T(8,128)} %get-tuple-element.4.adj_in, f32[16,128]{1,0:T(8,128)} %get-tuple-element.5.sens_in), custom_call_target="tpu_custom_call" | custom-call | tf_op jit(solution)/shard_map/pallas_call | solution.py:747

commit v4 on v3

--- a/solution.py
+++ b/solution.py
@@ -64,8 +64,8 @@
 def kernel(
     sizes,
     loads_in, disp_in, stiff_ref, col_in, face_in, zone_in,
-    adj_ref, sens_ref,
-    loads_ref, disp_ref, col_ref, face_ref, zone_ref,
+    adj_out, sens_out,
+    adj_ref, sens_ref, loads_ref, disp_ref, col_ref, face_ref, zone_ref,
     m_ref, w_ref,
     zf, zh, zl, wf, wh0, wl0,
     zp_ref, qs_ref, qp_ref, wp_ref, vp_ref,
@@ -75,7 +75,7 @@
     g1_ref, g2_ref, g1_slots, g2_slots,
     part_ref, carry_ref,
     load_sems, input_sems, z_send_sems, z_recv_sems, w_send_sems, w_recv_sems,
-    red_send_sems, red_recv_sems, carry_sems,
+    red_send_sems, red_recv_sems, carry_sems, out_sems,
 ):
     nx, ny, nz = sizes
     nb = ny * nz
@@ -663,13 +663,15 @@
     yh, ym, yl = thirds(both)
     lhs = jnp.concatenate([yh, yh, ym, yh, ym, yl], axis=1)
 
-    def finish(step, _):
-        lanes = pl.ds(pl.multiple_of(step * 512, 512), 512)
+    leaving = [pltpu.make_async_copy(sens_ref, sens_out, out_sems.at[8])]
+    sens_ref[...] = nn(lhs, sens_right)
+    leaving[0].start()
+    for step in range(8):
+        lanes = pl.ds(step * 512, 512)
         adj_ref[:, lanes] = nn(lhs, vp_ref[:, lanes])
-        return 0
-
-    lax.fori_loop(0, 8, finish, 0, unroll=8)
-    sens_ref[...] = nn(lhs, sens_right)
+        copy = pltpu.make_async_copy(adj_ref.at[:, lanes], adj_out.at[:, lanes], out_sems.at[step])
+        copy.start()
+        leaving.append(copy)
 
     for d in range(6):
         end_face(d, zline)
@@ -677,6 +679,8 @@
     red_all(0, g1_slots, along).wait_send()
     red_all(1, g2_slots, across).wait_send()
     carry.wait_send()
+    for copy in leaving:
+        copy.wait()
 
 
 def settle(adj_in, sens_in, adj_out, sens_out, adj_ref, sens_ref, sems):
@@ -701,7 +705,6 @@
     nb = ny * nz
     tiles = jnp.transpose(stiffness, (1, 0, 2)).reshape(7, 8, 8, 32, LANES)
     tiles = jnp.transpose(tiles, (0, 1, 3, 2, 4)).reshape(7 * 8 * 32 * 8, LANES)
-    vmem = pl.BlockSpec(memory_space=pltpu.VMEM)
     dma = pltpu.SemaphoreType.DMA
     v = pltpu.VMEM
     results = pl.pallas_call(
@@ -711,8 +714,9 @@
             jax.ShapeDtypeStruct((COLS, ZONE_DEV), F32),
         ),
         in_specs=[pl.BlockSpec(memory_space=pl.ANY)] * 6,
-        out_specs=(vmem, vmem),
+        out_specs=(pl.BlockSpec(memory_space=pl.ANY),) * 2,
         scratch_shapes=[
+            v((COLS, NODES * DOF), F32), v((COLS, ZONE_DEV), F32),
             v((COLS, NODES * DOF), F32), v((32, LANES), F32), pltpu.SMEM((7, NODES), jnp.int32),
             pltpu.SMEM((6, 16), jnp.int32), v((6, NODES), jnp.int32),
             v((7 * 8 * 32 * 8, LANES), F32), v((2 * NODES * DOF, 512), BF16),
@@ -731,7 +735,7 @@
             v((nx - 1, 8, LANES), F32), v((nb - 1, 8, LANES), F32),
             v((2 * COLS, ZONE_DEV), F32), v((2 * COLS, ZONE_DEV), F32),
             dma((7,)), dma((5,)), dma((6,)), dma((6,)), dma((6,)), dma((6,)),
-            dma((2,)), dma((2,)), dma((2,)),
+            dma((2,)), dma((2,)), dma((2,)), dma((9,)),
         ],
         compiler_params=pltpu.CompilerParams(
             collective_id=0, has_side_effects=True, vmem_limit_bytes=63 * 1024 * 1024

time: 40.5 us -> 40.5 us (level)
  no operation moved by 1% of the time
where the time goes in v4:
time: 40.5 us; the launch traced here: 40.3 us
  Pallas kernels  39.7 us (98%)
  between operations  0.64 us (2%)
    pallas_call x1, Pallas kernels, on_device(): pl.pallas_call(functools.partial(kernel, sizes), out_shape=(jax.ShapeDtyp...  38 us
    pallas_call x1, Pallas kernels, on_device(): pl.pallas_call(settle, out_shape=(jax.ShapeDtypeStruct((COLS, NODES * DOF...  1.66 us

profile of v4, /device:TPU:1, one launch (start us, length us, event | category | flops | bytes accessed | tf_op | source)
XLA Modules:
  0.0 40.3 jit_solution(7709699189414909562)
XLA Ops:
  0.6 38.0 %shard_map.77 = (f32[16,4096]{1,0:T(8,128)}, f32[16,128]{1,0:T(8,128)}) custom-call(f32[16,4096]{1,0:T(8,128)} %loads_in.1, f32[32,128]{1,0:T(8,128)} %bitcast.11, f32[14336,128]{1,0:T(8,128)} %bitcast.10, s32[7,64]{1,0:T(8,128)} %bitcast.12, s32[6,16]{1,0:T(8,128)} %face_in.1, s32[6,64]{1,0:T(8,128)} %bitcast.13), custom_call_target="tpu_custom_call" | custom-call | flops 400000000 | bytes 8000000 | tf_op jit(solution)/shard_map/pallas_call | solution.py:710
  38.7 1.7 %shard_map.78 = (f32[16,4096]{1,0:T(8,128)}, f32[16,128]{1,0:T(8,128)}) custom-call(f32[16,4096]{1,0:T(8,128)} %get-tuple-element.4.adj_in, f32[16,128]{1,0:T(8,128)} %get-tuple-element.5.sens_in), custom_call_target="tpu_custom_call" | custom-call | tf_op jit(solution)/shard_map/pallas_call | solution.py:751
